TPU v7x, 32 devices: a whole 2x2x4 slice. The times are simulated.
32 devices in a mesh: frames: 8 (over y, x, core), pairs: 4 (over z).
Axes of the slice: x: 2, y: 2, z: 4, core: 2. Of those that a mesh axis runs over, the one named last changes fastest.
Arguments:
- coords: float32 [5120, 3, 300], P('frames'), as said below
- centroids: float32 [384, 3, 300], P('frames'), as said below
- assignment: int32 [5120], P('frames'), may hold values from 0 to 383, as said below
- home_row: int32 [384], replicated, may hold values from 0 to 383, as said below
- pair_index: int32 [2, 45056], P(None, 'pairs'), may hold values from 0 to 299, as said below
- mean_dist: float32 [45056], P('pairs'), may hold values from 2 to 5
- tica_weight: bfloat16 [45056, 100], P('pairs'), may hold values from -0.02734375 to 0.02734375
Outputs:
- tica_proj: float32 [5120, 100], P('frames', 'pairs')
- new_centroids: float32 [384, 3, 300], P('frames')
- occupancy: float32 [384], P('frames')
Inputs may be any that keep to these rules, and one draw needn't show every extreme that they name: `assignment`: microstate m is kept by index home_row[m] // 48 of frames. The frames of one device (an aligned block of 640 rows) name microstates of any one such index at most 160 times, and of some index exactly 160 times, in every block. `home_row`: each number appears once. `pair_index`: the two residues of a pair differ. `coords`: positions in nanometres. `centroids`: positions in nanometres.
All inputs are finite; a program needn't handle non-finite values.
Results may differ from a plain program's by a relative error of at most 0.0029.
Values sent between devices are 32-bit elements; how exact they have to be, the bound alone decides.
No kernel may reach another device: no remote copies, remote signals or barrier semaphores. Data moves between devices by JAX's collectives and lax.ppermute only.
A program may use at most 128 MiB of HBM per device.

v0:
```python
import math

import jax
import jax.numpy as jnp
from jax import lax
from jax.sharding import PartitionSpec as P

NEWTON = 8


prior_weight = 4.0


def polar_factor(cross):
    scale = jnp.sqrt(jnp.sum(cross * cross, axis=(0, 1)))
    matrix = cross / scale
    for newton_step in range(NEWTON):
        entry = [[matrix[i, j] for j in range(3)] for i in range(3)]
        cofactor = [
            [
                entry[(i + 1) % 3][(j + 1) % 3] * entry[(i + 2) % 3][(j + 2) % 3]
                - entry[(i + 1) % 3][(j + 2) % 3] * entry[(i + 2) % 3][(j + 1) % 3]
                for j in range(3)
            ]
            for i in range(3)
        ]
        determinant = (
            entry[0][0] * cofactor[0][0]
            + entry[0][1] * cofactor[0][1]
            + entry[0][2] * cofactor[0][2]
        )
        stacked = jnp.stack([jnp.stack(line) for line in cofactor])
        matrix = 0.5 * (matrix + stacked / determinant)
    return matrix


def align_frames(centered, refs, valid):
    cross = jnp.einsum("bar,bcr->acb", refs, centered, precision=lax.Precision.HIGHEST)
    identity = jnp.eye(3, dtype=jnp.float32)[:, :, None]
    cross = jnp.where(valid[None, None, :], cross, identity)
    rotation = polar_factor(cross)
    return jnp.einsum("acb,bcr->bar", rotation, centered, precision=lax.Precision.HIGHEST)


def local(coords, centroids, assignment, home_row, pair_index, mean_dist, tica_weight):
    frames_local = coords.shape[0]
    res_count = coords.shape[2]
    comps = tica_weight.shape[1]
    block_rows = math.gcd(frames_local, 512)
    residue_ids = lax.broadcasted_iota(jnp.int32, (res_count, 1), 0)
    selector = (residue_ids == pair_index[0][None, :]).astype(jnp.float32) - (
        residue_ids == pair_index[1][None, :]
    ).astype(jnp.float32)

    def project_block(block):
        flat = block.reshape(block_rows * 3, res_count)
        diff = jnp.dot(
            flat, selector, precision=lax.Precision.HIGHEST, preferred_element_type=jnp.float32
        )
        diff = diff.reshape(block_rows, 3, -1)
        total = jnp.sum(diff * diff, axis=1)
        feature = (jnp.sqrt(total) - mean_dist[None, :]).astype(jnp.bfloat16)
        return jnp.dot(feature, tica_weight, preferred_element_type=jnp.float32)

    blocks = coords.reshape(frames_local // block_rows, block_rows, 3, res_count)
    partial_proj = lax.map(project_block, blocks).reshape(frames_local, comps)
    share = comps // lax.axis_size("pairs")
    full_proj = lax.psum(partial_proj, "pairs")
    square_mean = jnp.mean(full_proj * full_proj, axis=1)
    tica_part = lax.dynamic_slice_in_dim(full_proj, lax.axis_index("pairs") * share, share, 1)
    weight = 1.0 / (1.0 + 4.0 * square_mean)
    micro = home_row.shape[0]
    owners = lax.axis_size("frames")
    ms_local = centroids.shape[0]
    states = lax.broadcasted_iota(jnp.int32, (1, micro), 1)
    frame_row = jnp.sum(jnp.where(assignment[:, None] == states, home_row[None, :], 0), axis=1)
    centered = coords - jnp.mean(coords, axis=2, keepdims=True)
    ref_centered = centroids - jnp.mean(centroids, axis=2, keepdims=True)
    flat_centered = centered.reshape(frames_local, 3 * res_count)
    capacity = 2 * frames_local // owners
    owner_dev = frame_row // ms_local
    local_slot = frame_row % ms_local
    owner_ids = lax.broadcasted_iota(jnp.int32, (1, owners), 1)
    one_hot = (owner_dev[:, None] == owner_ids).astype(jnp.float32)
    row_ids = lax.broadcasted_iota(jnp.int32, (frames_local, frames_local), 0)
    col_ids = lax.broadcasted_iota(jnp.int32, (frames_local, frames_local), 1)
    lower = (row_ids >= col_ids).astype(jnp.float32)
    running = jnp.dot(lower, one_hot, preferred_element_type=jnp.float32)
    position = jnp.sum((running - 1.0) * one_hot, axis=1).astype(jnp.int32)
    target = owner_dev * capacity + position
    slot_line = lax.broadcasted_iota(jnp.int32, (owners * capacity, 1), 0)
    placement = (slot_line == target[None, :]).astype(jnp.float32)
    send_coords = jnp.dot(
        placement,
        flat_centered,
        precision=lax.Precision.HIGHEST,
        preferred_element_type=jnp.float32,
    )
    send_weight = jnp.dot(
        placement, weight, precision=lax.Precision.HIGHEST, preferred_element_type=jnp.float32
    )
    send_slot = jnp.dot(
        placement,
        local_slot.astype(jnp.float32),
        precision=lax.Precision.HIGHEST,
        preferred_element_type=jnp.float32,
    )
    send_coords = send_coords.reshape(owners, capacity, 3, res_count)
    send_weight = send_weight.reshape(owners, capacity)
    send_slot = send_slot.reshape(owners, capacity)
    ref_flat = ref_centered.reshape(ms_local, 3 * res_count)
    slot_row = lax.broadcasted_iota(jnp.int32, (1, ms_local), 1).astype(jnp.float32)
    got_coords = lax.all_to_all(send_coords, "frames", split_axis=0, concat_axis=0, tiled=True)
    got_weight = lax.all_to_all(send_weight, "frames", split_axis=0, concat_axis=0, tiled=True)
    got_slot = lax.all_to_all(send_slot, "frames", split_axis=0, concat_axis=0, tiled=True)
    lead, count = got_weight.shape
    flat_coords = got_coords.reshape(lead * count, 3, res_count)
    flat_weight = got_weight.reshape(lead * count)
    flat_slot = got_slot.reshape(lead * count)
    pick = (flat_slot[:, None] == slot_row).astype(jnp.float32)
    refs = jnp.dot(
        pick, ref_flat, precision=lax.Precision.HIGHEST, preferred_element_type=jnp.float32
    ).reshape(lead * count, 3, res_count)
    aligned = align_frames(flat_coords, refs, flat_weight > 0.0)
    weighted = (flat_weight[:, None, None] * aligned).reshape(lead, count, 3, res_count)
    weighted, got_weight, got_slot = (weighted, got_weight, got_slot)
    slot_ids = lax.broadcasted_iota(jnp.int32, (ms_local, 1), 0).astype(jnp.float32)
    member = (got_slot.reshape(1, -1) == slot_ids).astype(jnp.float32)
    summed = jnp.dot(
        member, weighted.reshape(-1, 3 * res_count), precision=lax.Precision.HIGHEST
    ).reshape(ms_local, 3, res_count)
    occupancy = jnp.dot(member, got_weight.reshape(-1), precision=lax.Precision.HIGHEST)
    new_centroids = (prior_weight * ref_centered + summed) / (
        prior_weight + occupancy[:, None, None]
    )
    return (tica_part, new_centroids, occupancy)


def solution(mesh):
    in_specs = (
        P("frames", None, None),
        P("frames", None, None),
        P("frames"),
        P(),
        P(None, "pairs"),
        P("pairs"),
        P("pairs", None),
    )
    out_specs = (P("frames", "pairs"), P("frames", None, None), P("frames"))
    return jax.shard_map(local, mesh=mesh, in_specs=in_specs, out_specs=out_specs, check_vma=False)
```

profile of v0, /device:TPU:0, one launch (start us, length us, event | category | flops | bytes accessed | tf_op | source)
XLA Modules:
  0.0 507.7 jit_solution(3651047952975017152)
XLA Ops:
  10.7 5.2 %all-to-all-start = ((f32[8,1,160]{2,1,0:T(1,128)}), f32[8,1,160]{2,1,0:T(1,128)S(1)}, u32[]{:S(2)}, u32[]{:S(2)}) async-start(f32[8,1,160]{2,1,0:T(1,128)} %all_to_all.15), calls=%async_computation | async-start | bytes 16384 | tf_op jit(solution)/shard_map/all_to_all | solution.py:115
  17.0 4.6 copy.173
  21.6 4.5 copy.174
  26.1 238.5 %while.11 = (s32[]{:T(128)}, f32[5,128,100]{1,2,0:T(8,128)S(1)}, f32[5,128,3,300]{1,3,2,0:T(8,128)}, f32[11264]{0:T(1024)S(1)}, bf16[11264,100]{0,1:T(8,128)(2,1...) while((s32[]{:T(128)}, f32[5,128,100]{1,2,0:T(8,128)S(1)}, ...), condition=%wide.region_2.3_spmd.clone, body=%wide.region_0.2_spmd.clone.sunk | while | flops 15886700544 | bytes 14532709 | solution.py:66
  26.3 45.7 %fusion.82 = f32[128,11264]{1,0:T(8,128)S(1)} fusion(s32[11264]{0:T(1024)S(1)} %get-tuple-element.267, s32[11264]{0:T(1024)S(1)} %get-tuple-element.266, f32[5,128,3,300]{1,3,2,0:T(8,128)} %get-tuple-element.263, s32[]{:T(128)S(6)} %copy.199), kind=kOutput, calls=%fused_computation.11.clone.1 | convolution fusion | flops 15595458560 | bytes 6324228 | tf_op jit(solution)/shard_map/while/body/eval_jaxpr/dot_general | solution.py:57
  72.0 1.9 fusion.83
  73.9 45.7 %fusion.82 = f32[128,11264]{1,0:T(8,128)S(1)} fusion(s32[11264]{0:T(1024)S(1)} %get-tuple-element.267, s32[11264]{0:T(1024)S(1)} %get-tuple-element.266, f32[5,128,3,300]{1,3,2,0:T(8,128)} %get-tuple-element.263, s32[]{:T(128)S(6)} %copy.199), kind=kOutput, calls=%fused_computation.11.clone.1 | convolution fusion | flops 15595458560 | bytes 6324228 | tf_op jit(solution)/shard_map/while/body/eval_jaxpr/dot_general | solution.py:57
  119.6 1.9 fusion.83
  121.5 45.7 %fusion.82 = f32[128,11264]{1,0:T(8,128)S(1)} fusion(s32[11264]{0:T(1024)S(1)} %get-tuple-element.267, s32[11264]{0:T(1024)S(1)} %get-tuple-element.266, f32[5,128,3,300]{1,3,2,0:T(8,128)} %get-tuple-element.263, s32[]{:T(128)S(6)} %copy.199), kind=kOutput, calls=%fused_computation.11.clone.1 | convolution fusion | flops 15595458560 | bytes 6324228 | tf_op jit(solution)/shard_map/while/body/eval_jaxpr/dot_general | solution.py:57
  167.2 1.9 fusion.83
  169.1 45.7 %fusion.82 = f32[128,11264]{1,0:T(8,128)S(1)} fusion(s32[11264]{0:T(1024)S(1)} %get-tuple-element.267, s32[11264]{0:T(1024)S(1)} %get-tuple-element.266, f32[5,128,3,300]{1,3,2,0:T(8,128)} %get-tuple-element.263, s32[]{:T(128)S(6)} %copy.199), kind=kOutput, calls=%fused_computation.11.clone.1 | convolution fusion | flops 15595458560 | bytes 6324228 | tf_op jit(solution)/shard_map/while/body/eval_jaxpr/dot_general | solution.py:57
  214.8 1.9 fusion.83
  216.7 45.7 %fusion.82 = f32[128,11264]{1,0:T(8,128)S(1)} fusion(s32[11264]{0:T(1024)S(1)} %get-tuple-element.267, s32[11264]{0:T(1024)S(1)} %get-tuple-element.266, f32[5,128,3,300]{1,3,2,0:T(8,128)} %get-tuple-element.263, s32[]{:T(128)S(6)} %copy.199), kind=kOutput, calls=%fused_computation.11.clone.1 | convolution fusion | flops 15595458560 | bytes 6324228 | tf_op jit(solution)/shard_map/while/body/eval_jaxpr/dot_general | solution.py:57
  262.4 1.9 fusion.83
  265.6 1.8 reduce_sum.67
  269.0 1.7 reshape.3015
  270.7 1.6 reshape.3024
  272.3 31.5 %all-reduce.2.cloned.1.call-done = f32[640,100]{1,0:T(8,128)} async-done(((f32[640,100]{1,0:T(8,128)}), f32[640,100]{1,0:T(8,128)}) %all-reduce.2.cloned.1.call-update) | async-done | bytes 256016 | tf_op jit(solution)/shard_map/psum | solution.py:68
  307.1 3.7 all-to-all-start.1
  310.8 11.4 %fusion.27 = f32[8,160,3,300]{3,1,2,0:T(8,128)} fusion(f32[3,300,640,1]{2,1,0,3:T(8,128)} %reshape.3024, s32[640]{0:T(1024)S(1)} %get-tuple-element.196, s32[8,160]{1,0:T(8,128)S(1)} %multiply_add_fusion), kind=kOutput, calls=%fused_computation.27 | convolution fusion | flops 8848179200 | bytes 6919680 | tf_op jit(solution)/shard_map/dot_general | solution.py:93
  322.1 4.9 all-to-all-start.2
  327.9 4.2 fusion.42
  332.0 9.0 %copy.180 = f32[1280,3,300]{2,1,0:T(4,128)} copy(f32[1280,3,300]{0,2,1:T(8,128)} %fusion.42) | data formatting | bytes 9216000 | tf_op jit(solution)/shard_map/dot_general | solution.py:121
  343.0 51.4 %all-to-all-done.2 = f32[8,160,3,300]{3,1,2,0:T(8,128)} async-done(((f32[8,160,3,300]{3,1,2,0:T(8,128)}), f32[8,160,3,300]{3,1,2,0:T(8,128)}, u32[]{:S(2)}, u32[]{:S(2)}) %all-to-all-start.2) | async-done | bytes 4608032 | tf_op jit(solution)/shard_map/all_to_all | solution.py:113
  394.4 3.2 copy.176
  397.6 2.8 copy-done
  401.2 42.0 %fusion.20 = f32[1280,3,3]{2,1,0:T(4,128)S(1)} fusion(f32[1280,3,300]{2,1,0:T(4,128)S(1)} %copy-done.2, f32[1280,3,300]{2,0,1:T(8,128)S(1)} %bitcast.243), kind=kOutput, calls=%fused_computation.21 | convolution fusion | flops 41472000 | bytes 9262080 | tf_op jit(solution)/shard_map/bar,bcr->acb/dot_general | solution.py:38
  448.1 27.3 %fusion.22 = f32[1280,3,300]{2,1,0:T(4,128)} fusion(f32[3,3,1280]{1,0,2:T(4,128)S(1)} %copy.182, f32[1280,3,300]{2,0,1:T(8,128)} %bitcast.244, f32[1280]{0:T(1024)S(1)} %mul.1808), kind=kOutput, calls=%fused_computation.23 | convolution fusion | flops 42624000 | bytes 9267200 | tf_op jit(solution)/shard_map/acb,bcr->bar/dot_general | solution.py:42
  475.4 9.9 %reshape.3032 = f32[1280,900]{1,0:T(8,128)} reshape(f32[1280,3,300]{2,1,0:T(4,128)} %fusion.22) | data formatting | bytes 9216000 | tf_op jit(solution)/shard_map/reshape;reshape | solution.py:130
  485.3 5.7 %copy.187 = f32[1280,900]{0,1:T(8,128)} copy(f32[1280,900]{1,0:T(8,128)} %reshape.3032) | data formatting | bytes 9216000 | tf_op jit(solution)/shard_map/reshape;reshape | solution.py:130
  491.0 4.3 dot_general.59
  495.2 5.4 %fusion.35 = f32[48,3,300]{2,0,1:T(8,128)} fusion(f32[3,300,1280]{2,1,0:T(8,128)} %dot_general.59, f32[48,3,300]{2,0,1:T(8,128)S(1)} %broadcast_subtract_fusion.1, f32[1280]{0:T(1024)S(1)} %eq.140, f32[48]{0:T(128)S(1)} %iota_convert_fusion, f32[48]{0:T(128)S(1)} %get-tuple-element.198), kind=kOutput, calls=%fused_computation.38 | convolution fusion | flops 663743040 | bytes 4959104 | tf_op jit(solution)/shard_map/dot_general | solution.py:129
  (104 shorter events, 18.6 us)
Async XLA Ops:
  10.7 296.4 %all-to-all-start = ((f32[8,1,160]{2,1,0:T(1,128)}), f32[8,1,160]{2,1,0:T(1,128)S(1)}, u32[]{:S(2)}, u32[]{:S(2)}) async-start(f32[8,1,160]{2,1,0:T(1,128)} %all_to_all.15), calls=%async_computation | async-start | bytes 16384 | tf_op jit(solution)/shard_map/all_to_all | solution.py:115
  15.9 287.8 %all-reduce.2.cloned.1.call-start = ((), (), s32[]{:S(2)}) async-start(), calls=%async_computation.3 | async-start | bytes 655360 | tf_op jit(solution)/shard_map/psum | solution.py:68
  17.0 9.2 %copy-start.1 = (bf16[11264,100]{0,1:T(8,128)(2,1)S(1)}, bf16[11264,100]{0,1:T(8,128)(2,1)}, u32[]{:S(2)}) copy-start(bf16[11264,100]{0,1:T(8,128)(2,1)} %param.15) | copy-start | bytes 6758404
  17.0 9.1 %copy-start.5 = (f32[11264]{0:T(1024)S(1)}, f32[11264]{0:T(1024)}, u32[]{:S(2)}) copy-start(f32[11264]{0:T(1024)} %param.14) | copy-start | bytes 135172
  264.7 2.7 copy-start.3
  307.1 15.0 %all-to-all-start.1 = ((f32[8,1,160]{2,1,0:T(1,128)}), f32[8,1,160]{2,1,0:T(1,128)S(1)}, u32[]{:S(2)}, u32[]{:S(2)}) async-start(f32[8,1,160]{2,1,0:T(1,128)} %all_to_all.17), calls=%async_computation.1 | async-start | bytes 16384 | tf_op jit(solution)/shard_map/all_to_all | solution.py:114
  322.1 4.9 copy-start.6
  322.1 72.2 %all-to-all-start.2 = ((f32[8,160,3,300]{3,1,2,0:T(8,128)}), f32[8,160,3,300]{3,1,2,0:T(8,128)}, u32[]{:S(2)}, u32[]{:S(2)}) async-start(f32[8,160,3,300]{3,1,2,0:T(8,128)} %fusion.27), calls=%async_computation.2 | async-start | bytes 11796480 | tf_op jit(solution)/shard_map/all_to_all | solution.py:113
  332.0 9.0 %copy-start.4 = (f32[640,100]{1,0:T(8,128)S(1)}, f32[640,100]{1,0:T(8,128)}, u32[]{:S(2)}) copy-start(f32[640,100]{1,0:T(8,128)} %all-reduce.2.cloned.1.call-done) | copy-start | bytes 768004
  394.4 6.8 %copy-start.2 = (f32[1280,3,300]{2,1,0:T(4,128)S(1)}, f32[1280,3,300]{2,1,0:T(4,128)}, u32[]{:S(2)}) copy-start(f32[1280,3,300]{2,1,0:T(4,128)} %copy.180) | copy-start | bytes 13824004
  397.6 2.9 copy-start
Sparse Core Ops, SparseCore 0:
  265.8 37.9 all-reduce.1
where the time goes:
time: 511 us; the launch traced here: 508 us
  matrix products  332 us (65%)
  waiting for transfers between devices  82.8 us (16%)
  local copies, waits for them, and re-layouts  55.1 us (11%)
  between operations  14.8 us (3%)
  starting transfers between devices  13.7 us (3%)
  other arithmetic  8.35 us (2%)
    dot_general x5, matrix products, project_block(): jnp.dot(flat, selector, precision=lax.Precision.HIGHEST, preferred_elemen...  228 us
    all_to_all x1, waiting for transfers between devices, local(): lax.all_to_all(send_coords, 'frames', split_axis=0, concat_axis=0, tiled=...  51.4 us
    dot_general x1, matrix products, align_frames(): jnp.einsum('bar,bcr->acb', refs, centered, precision=lax.Precision.HIGHEST)  42 us
    psum x1, waiting for transfers between devices, local(): full_proj = lax.psum(partial_proj, 'pairs')  31.5 us
    dot_general x1, matrix products, align_frames(): jnp.einsum('acb,bcr->bar', rotation, centered, precision=lax.Precision.HI...  27.3 us
    another operation x2, local copies, waits for them, and re-layouts, local(): weighted.reshape(-1, 3 * res_count)  15.6 us
    unnamed x17, local copies, waits for them, and re-layouts  13.5 us
    dot_general x1, matrix products, local(): jnp.dot(placement, flat_centered, precision=lax.Precision.HIGHEST, prefer...  11.4 us
  transfers between devices with their start and end apart: 4, of which 2 were waited for; matrix products, arithmetic and copies ran while one was open for 56% of the time, Pallas kernels for 0%

commit v1 on v0

v1 whole, which is shorter than its diff:
```python
import functools

import jax
import jax.numpy as jnp
from jax import lax
from jax.experimental import pallas as pl
from jax.experimental.pallas import tpu as pltpu
from jax.sharding import PartitionSpec as P

NEWTON = 8
PIECES = 3
VMEM_BYTES = 60 * 2**20

prior_weight = 4.0
piece_type = jnp.float8_e4m3fn


def round_up(value, multiple):
    return -(-value // multiple) * multiple


def center_rows(rows):
    return rows - jnp.sum(rows, axis=0, keepdims=True) / rows.shape[0]


def load_pieces(coords_ref, split_ref, positions_ref, unit_ref, stride):
    dims, res_count, frames = coords_ref.shape
    centered = [center_rows(coords_ref[c]) for c in range(dims)]
    reach = functools.reduce(
        jnp.maximum, [jnp.max(jnp.abs(rows), axis=0, keepdims=True) for rows in centered]
    )
    reach = jnp.maximum(reach, 1e-30)
    unit_ref[...] = jnp.broadcast_to(reach * (1.0 / 256.0), (128, frames)).T
    scale = 256.0 / reach
    split_ref[...] = jnp.zeros_like(split_ref)
    for c in range(dims):
        rest = centered[c] * scale
        for k in range(PIECES):
            piece = rest.astype(piece_type).astype(jnp.float32)
            split_ref[k * stride : k * stride + res_count, :] = piece
            rest = rest - piece
        positions_ref[c * frames : (c + 1) * frames, :] = split_ref[...].T.astype(piece_type)


def project_kernel(
    axis, share, index_ref, mean_ref, weight_ref, coords_ref, *refs
):
    out_refs = refs[:-5]
    split_ref, positions_ref, unit_ref, selector_ref, total_ref = refs[-5:]
    dims, res_count, frames = coords_ref.shape
    comps, pairs = weight_ref.shape
    step = pl.program_id(0)
    stride = round_up(res_count, 32)

    @pl.when(step == 0)
    def _():
        load_pieces(coords_ref, split_ref, positions_ref, unit_ref, stride)
        total_ref[...] = jnp.zeros_like(total_ref)
        selector_ref[...] = jnp.zeros_like(selector_ref)

    residue = lax.broadcasted_iota(jnp.int32, (stride, pairs), 0)
    selector = (
        jnp.where(residue == index_ref[0:1, :], 1.0, 0.0)
        - jnp.where(residue == index_ref[1:2, :], 1.0, 0.0)
    ).astype(piece_type)
    for k in range(PIECES):
        selector_ref[k * stride : (k + 1) * stride, :] = selector
    square = None
    for c in range(dims):
        diff = jnp.dot(
            positions_ref[c * frames : (c + 1) * frames, :],
            selector_ref[...],
            preferred_element_type=jnp.float32,
        )
        square = diff * diff if square is None else square + diff * diff
    distance = square * lax.rsqrt(jnp.maximum(square, 1e-37)) * unit_ref[:, 0:1]
    feature = (distance - mean_ref[0:1, :]).astype(jnp.bfloat16)
    total_ref[:, 0:comps] += lax.dot_general(
        feature,
        weight_ref[...],
        (((1,), (1,)), ((), ())),
        preferred_element_type=jnp.float32,
    )

    @pl.when(step == pl.num_programs(0) - 1)
    def _():
        flipped = total_ref[...].T
        parts = len(out_refs)
        rows = [flipped[k * share : (k + 1) * share, :] for k in range(parts)]
        me = lax.axis_index(axis)
        for s, out_ref in enumerate(out_refs):
            owner = lax.rem(me + s, parts)
            value = rows[0]
            for k in range(1, parts):
                value = jnp.where(owner == k, rows[k], value)
            out_ref[...] = value


def project(coords, pair_index, mean_dist, tica_weight, axis):
    dims, res_count, frames = coords.shape
    comps, pairs = tica_weight.shape
    parts = lax.axis_size(axis)
    share = comps // parts
    block = next(b for b in (2816, 1408, 1024, 512, 256, 128, pairs) if pairs % b == 0)
    depth = round_up(PIECES * round_up(res_count, 32), 256)
    return pl.pallas_call(
        functools.partial(project_kernel, axis, share),
        grid=(pairs // block,),
        in_specs=[
            pl.BlockSpec((2, block), lambda i: (0, i)),
            pl.BlockSpec((1, block), lambda i: (0, i)),
            pl.BlockSpec((comps, block), lambda i: (0, i)),
            pl.BlockSpec((dims, res_count, frames), lambda i: (0, 0, 0)),
        ],
        out_specs=[pl.BlockSpec((share, frames), lambda i: (0, 0))] * parts,
        out_shape=[jax.ShapeDtypeStruct((share, frames), jnp.float32)] * parts,
        scratch_shapes=[
            pltpu.VMEM((depth, frames), jnp.float32),
            pltpu.VMEM((dims * frames, depth), piece_type),
            pltpu.VMEM((frames, 128), jnp.float32),
            pltpu.VMEM((depth, block), piece_type),
            pltpu.VMEM((frames, round_up(comps, 128)), jnp.float32),
        ],
        compiler_params=pltpu.CompilerParams(vmem_limit_bytes=VMEM_BYTES),
        cost_estimate=pl.CostEstimate(
            flops=2 * dims * frames * pairs * depth, bytes_accessed=8 * 2**20, transcendentals=0
        ),
        name="project",
    )(pair_index, mean_dist, tica_weight, coords)


def polar_factor(cross):
    size = sum(cross[i][j] * cross[i][j] for i in range(3) for j in range(3))
    size = jnp.sqrt(size)
    entry = [[cross[i][j] / size for j in range(3)] for i in range(3)]
    for newton_step in range(NEWTON):
        cofactor = [
            [
                entry[(i + 1) % 3][(j + 1) % 3] * entry[(i + 2) % 3][(j + 2) % 3]
                - entry[(i + 1) % 3][(j + 2) % 3] * entry[(i + 2) % 3][(j + 1) % 3]
                for j in range(3)
            ]
            for i in range(3)
        ]
        determinant = (
            entry[0][0] * cofactor[0][0]
            + entry[0][1] * cofactor[0][1]
            + entry[0][2] * cofactor[0][2]
        )
        inverse = 1.0 / determinant
        entry = [
            [0.5 * (entry[i][j] + cofactor[i][j] * inverse) for j in range(3)] for i in range(3)
        ]
    return entry


def align_kernel(frames_axis, pairs_axis, quarter, coords_ref, assigned_ref, home_ref, *refs):
    parts = len(refs) - 4
    piece_refs = refs[:parts]
    member_ref, aligned_ref, refs_ref, centered_ref = refs[parts:]
    dims, res_count, frames = coords_ref.shape
    micro = home_ref.shape[1]
    local_micro = piece_refs[0].shape[1]
    me = lax.axis_index(frames_axis)
    for s, piece_ref in enumerate(piece_refs):
        owner = lax.rem(me + parts - s, parts)
        at = pl.multiple_of(owner * local_micro, 8)
        refs_ref[:, pl.ds(at, local_micro), :] = piece_ref[...]

    state = lax.broadcasted_iota(jnp.int32, (micro, frames), 0)
    chosen = (state == assigned_ref[...]).astype(jnp.float32).astype(jnp.bfloat16)
    home = home_ref[...]
    half = lax.broadcasted_iota(jnp.int32, (16, micro), 0)
    halves = jnp.where(half == 0, home >> 5, jnp.where(half == 1, home & 31, 0))
    picked = jnp.dot(
        halves.astype(jnp.float32).astype(jnp.bfloat16), chosen, preferred_element_type=jnp.float32
    )
    frame_row = (picked[0:1, :] * 32.0 + picked[1:2, :]).astype(jnp.int32)
    member = (state == frame_row).astype(jnp.float32).astype(jnp.bfloat16)
    member_ref[...] = member

    centered = [center_rows(coords_ref[c]) for c in range(dims)]
    centered_ref[...] = jnp.zeros_like(centered_ref)
    for c in range(dims):
        centered_ref[c, 0:res_count, :] = centered[c]
    cross = []
    for a in range(dims):
        rows = refs_ref[a]
        rows = (rows - jnp.sum(rows, axis=1, keepdims=True) / res_count).T
        high = rows.astype(jnp.bfloat16)
        low = (rows - high.astype(jnp.float32)).astype(jnp.bfloat16)
        own = jnp.dot(high, member, preferred_element_type=jnp.float32) + jnp.dot(
            low, member, preferred_element_type=jnp.float32
        )
        cross.append([jnp.sum(own * centered[b], axis=0, keepdims=True) for b in range(dims)])
    rotation = polar_factor(cross)
    start = pl.multiple_of(lax.axis_index(pairs_axis) * quarter, 8)
    mine = [centered_ref[b, pl.ds(start, quarter), :] for b in range(dims)]
    for a in range(dims):
        aligned_ref[a * quarter : (a + 1) * quarter, :] = sum(
            rotation[a][b] * mine[b] for b in range(dims)
        )


def align(coords, assignment, home_row, pieces, frames_axis, pairs_axis, quarter):
    dims, res_count, frames = coords.shape
    micro = home_row.shape[1]
    whole = quarter * lax.axis_size(pairs_axis)
    return pl.pallas_call(
        functools.partial(align_kernel, frames_axis, pairs_axis, quarter),
        out_shape=[
            jax.ShapeDtypeStruct((micro, frames), jnp.bfloat16),
            jax.ShapeDtypeStruct((dims * quarter, frames), jnp.float32),
        ],
        scratch_shapes=[
            pltpu.VMEM((dims, micro, res_count), jnp.float32),
            pltpu.VMEM((dims, whole, frames), jnp.float32),
        ],
        compiler_params=pltpu.CompilerParams(vmem_limit_bytes=VMEM_BYTES),
        cost_estimate=pl.CostEstimate(
            flops=8 * dims * frames * micro * res_count, bytes_accessed=2**22, transcendentals=0
        ),
        name="align",
    )(coords, assignment, home_row, *pieces)


def gather_kernel(axis, comps, member_ref, aligned_ref, *refs):
    square_refs = refs[:-3]
    out_ref, square_ref, weighted_ref = refs[-3:]
    parts = len(square_refs)
    me = lax.axis_index(axis)
    for s, ref in enumerate(square_refs):
        square_ref[lax.rem(me + parts - s, parts)] = ref[...]
    square = sum(square_ref[k] for k in range(parts))
    weight = 1.0 / (1.0 + 4.0 * (square / comps))
    rows = aligned_ref.shape[0]
    width, frames = weighted_ref.shape
    weighted_ref[0:rows, :] = aligned_ref[...] * weight
    tail = lax.broadcasted_iota(jnp.int32, (width - rows, frames), 0)
    weighted_ref[rows:, :] = jnp.where(tail == 0, weight, 0.0)
    weighted = weighted_ref[...]
    high = weighted.astype(jnp.bfloat16)
    low = (weighted - high.astype(jnp.float32)).astype(jnp.bfloat16)
    member = member_ref[...]
    over_frames = (((1,), (1,)), ((), ()))
    summed = lax.dot_general(
        member, high, over_frames, preferred_element_type=jnp.float32
    ) + lax.dot_general(member, low, over_frames, preferred_element_type=jnp.float32)
    out_ref[...] = summed.reshape(out_ref.shape)


def gather(member, aligned, squares, axis, comps, owners):
    micro, frames = member.shape
    rows = aligned.shape[0]
    width = round_up(rows + 1, 128)
    return pl.pallas_call(
        functools.partial(gather_kernel, axis, comps),
        out_shape=jax.ShapeDtypeStruct((owners, micro // owners, width), jnp.float32),
        scratch_shapes=[
            pltpu.VMEM((len(squares), 1, frames), jnp.float32),
            pltpu.VMEM((width, frames), jnp.float32),
        ],
        compiler_params=pltpu.CompilerParams(vmem_limit_bytes=VMEM_BYTES),
        name="gather",
    )(member, aligned, *squares)


def update_kernel(axis, quarter, centroids_ref, *refs):
    piece_refs = refs[:-3]
    out_ref, occupancy_ref, pieces_ref = refs[-3:]
    parts = len(piece_refs)
    dims, states, res_count = centroids_ref.shape
    me = lax.axis_index(axis)
    for s, ref in enumerate(piece_refs):
        pieces_ref[lax.rem(me + parts - s, parts)] = ref[...]
    occupancy = pieces_ref[0][:, dims * quarter : dims * quarter + 1]
    row = lax.broadcasted_iota(jnp.int32, (states, states), 0)
    column = lax.broadcasted_iota(jnp.int32, (states, states), 1)
    occupancy_ref[...] = jnp.sum(jnp.where(row == column, occupancy, 0.0), axis=0, keepdims=True)
    divisor = prior_weight + occupancy
    for c in range(dims):
        rows = centroids_ref[c]
        rows = rows - jnp.sum(rows, axis=1, keepdims=True) / res_count
        for z in range(parts):
            low, high = z * quarter, min((z + 1) * quarter, res_count)
            summed = pieces_ref[z][:, c * quarter : c * quarter + high - low]
            out_ref[c, :, low:high] = (prior_weight * rows[:, low:high] + summed) / divisor


def update(centroids, pieces, axis, quarter):
    dims, states, res_count = centroids.shape
    return pl.pallas_call(
        functools.partial(update_kernel, axis, quarter),
        out_shape=[
            jax.ShapeDtypeStruct((dims, states, res_count), jnp.float32),
            jax.ShapeDtypeStruct((1, states), jnp.float32),
        ],
        scratch_shapes=[pltpu.VMEM((len(pieces),) + pieces[0].shape, jnp.float32)],
        compiler_params=pltpu.CompilerParams(vmem_limit_bytes=VMEM_BYTES),
        name="update",
    )(centroids, *pieces)


def from_behind(value, axis, step):
    size = lax.axis_size(axis)
    return lax.ppermute(value, axis, [(i, (i + step) % size) for i in range(size)])


def gathered(value, axis):
    return [value] + [from_behind(value, axis, s) for s in range(1, lax.axis_size(axis))]


def local(coords, centroids, assignment, home_row, pair_index, mean_dist, tica_weight):
    comps = tica_weight.shape[1]
    parts = lax.axis_size("pairs")
    owners = lax.axis_size("frames")
    coords = jnp.transpose(coords, (1, 2, 0))
    centroids = jnp.transpose(centroids, (1, 0, 2))
    quarter = round_up(-(-coords.shape[1] // parts), 8)

    refs = gathered(centroids, "frames")
    partial = project(coords, pair_index, mean_dist[None, :], tica_weight.T, "pairs")
    tica = partial[0]
    for s in range(1, parts):
        tica = tica + from_behind(partial[s], "pairs", s)
    member, aligned = align(
        coords, assignment[None, :], home_row[None, :], refs, "frames", "pairs", quarter
    )
    squares = gathered(jnp.sum(tica * tica, axis=0, keepdims=True), "pairs")
    sums = gather(member, aligned, squares, "pairs", comps, owners)
    sums = lax.all_to_all(sums, "frames", split_axis=0, concat_axis=0, tiled=True)
    sums = jnp.sum(sums, axis=0)
    new_centroids, occupancy = update(centroids, gathered(sums, "pairs"), "pairs", quarter)
    return (tica.T, jnp.transpose(new_centroids, (1, 0, 2)), occupancy[0])


def solution(mesh):
    in_specs = (
        P("frames", None, None),
        P("frames", None, None),
        P("frames"),
        P(),
        P(None, "pairs"),
        P("pairs"),
        P("pairs", None),
    )
    out_specs = (P("frames", "pairs"), P("frames", None, None), P("frames"))
    return jax.shard_map(local, mesh=mesh, in_specs=in_specs, out_specs=out_specs, check_vma=False)
```

time: 511 us -> 104 us (0.20)
  matrix products: 332 us -> 0 us
  waiting for transfers between devices: 82.8 us -> 19.4 us
  local copies, waits for them, and re-layouts: 55.1 us -> 3.76 us
  Pallas kernels: 0 us -> 43.5 us
  between operations: 14.8 us -> 0.79 us
  blocking collectives: 0 us -> 11.7 us
  starting transfers between devices: 13.7 us -> 23.3 us
  other arithmetic: 8.35 us -> 1.66 us
    dot_general x19 -> x0, matrix products: 332 us -> none  [the longest x5 228 us: project_block(): jnp.dot(flat, selector, precision=lax.Precision.HIGHEST, preferred_elemen...]
    all_to_all x3 -> x0, waiting for transfers between devices: 51.4 us -> none  [the longest x1 51.4 us: local(): lax.all_to_all(send_coords, 'frames', split_axis=0, concat_axis=0, tiled=...]
    pallas_call x0 -> x4, Pallas kernels: none -> 43.5 us  [the longest x1 32.9 us: project(): pl.pallas_call(functools.partial(project_kernel, axis, share), grid=(pair...]
    psum x1 -> x0, waiting for transfers between devices: 31.5 us -> none  [local(): full_proj = lax.psum(partial_proj, 'pairs')]
    ppermute x0 -> x16, starting transfers between devices: none -> 23.3 us  [from_behind(): lax.ppermute(value, axis, [(i, (i + step) % size) for i in range(size)])]
    ppermute x0 -> x16, waiting for transfers between devices: none -> 19.4 us  [from_behind(): lax.ppermute(value, axis, [(i, (i + step) % size) for i in range(size)])]
    dot_general x5 -> x0, local copies, waits for them, and re-layouts: 16.1 us -> none  [the longest x2 9.23 us: local(): jnp.dot(pick, ref_flat, precision=lax.Precision.HIGHEST, preferred_elemen...]
    another operation x2 -> x0, local copies, waits for them, and re-layouts: 15.6 us -> none  [local(): weighted.reshape(-1, 3 * res_count)]
  transfers between devices with their start and end apart: 4 -> 16, of which waited for: 2 -> 6; matrix products, arithmetic and copies ran while one was open for 56% -> 3% of each run, Pallas kernels for 0% -> 38%
where the time goes in v1:
time: 104 us
  Pallas kernels  43.5 us (42%)
  starting transfers between devices  23.3 us (22%)
  waiting for transfers between devices  19.4 us (19%)
  blocking collectives  11.7 us (11%)
  local copies, waits for them, and re-layouts  3.76 us (4%)
  other arithmetic  1.66 us (2%)
    pallas_call x1, Pallas kernels, project(): pl.pallas_call(functools.partial(project_kernel, axis, share), grid=(pair...  32.9 us
    ppermute x16, starting transfers between devices, from_behind(): lax.ppermute(value, axis, [(i, (i + step) % size) for i in range(size)])  23.3 us
    ppermute x16, waiting for transfers between devices, from_behind(): lax.ppermute(value, axis, [(i, (i + step) % size) for i in range(size)])  19.4 us
    all_to_all x1, blocking collectives, local(): lax.all_to_all(sums, 'frames', split_axis=0, concat_axis=0, tiled=True)  11.7 us
    pallas_call x1, Pallas kernels, align(): pl.pallas_call(functools.partial(align_kernel, frames_axis, pairs_axis, q...  6.07 us
    unnamed x36, local copies, waits for them, and re-layouts  2.57 us
    pallas_call x1, Pallas kernels, gather(): pl.pallas_call(functools.partial(gather_kernel, axis, comps), out_shape=j...  2.5 us
  transfers between devices with their start and end apart: 16, of which 6 were waited for; matrix products, arithmetic and copies ran while one was open for 3% of the time, Pallas kernels for 38%

profile of v1, /device:TPU:0, one launch (start us, length us, event | category | flops | bytes accessed | tf_op | source)
XLA Modules:
  0.0 104.0 jit_solution(17257142455370241033)
XLA Ops:
  0.6 3.4 %collective-permute-start.9 = (f32[3,48,300]{2,1,0:T(8,128)}, f32[3,48,300]{2,1,0:T(8,128)S(1)}, u32[]{:S(2)}, u32[]{:S(2)}) collective-permute-start(f32[3,48,300]{2,1,0:T(8,128)} %bitcast.7), channel_id=1, source_target_pairs={{0,28},{4,0},{8,4},{12,8},{16,12},{20,16},{24,20},{28,24},{1,29},{... | collective-permute-start | bytes 518408 | tf_op jit(solution)/shard_map/ppermute | solution.py:306
  4.0 0.6 collective-permute-start.8
  4.7 32.9 %project.1 = (f32[25,640]{1,0:T(8,128)}, f32[25,640]{1,0:T(8,128)}, f32[25,640]{1,0:T(8,128)}, f32[25,640]{1,0:T(8,128)}) custom-call(s32[2,11264]{1,0:T(2,128)} %index_ref.1, f32[1,11264]{1,0:T(1,128)} %bitcast.21, bf16[100,11264]{1,0:T(8,128)(2,1)} %bitcast.17, f32[3,300,640]{2,1,0:T(8,128)} %bitcast.18), custom_call_target="tpu_custom_call" | custom-call | flops 44291850240 | bytes 8388608 | tf_op jit(solution)/shard_map/project/pallas_call | solution.py:106
  37.6 1.6 %collective-permute-start = (f32[25,640]{1,0:T(8,128)}, f32[25,640]{1,0:T(8,128)S(1)}, u32[]{:S(2)}, u32[]{:S(2)}) collective-permute-start(f32[25,640]{1,0:T(8,128)} %get-tuple-element.12), channel_id=1, source_target_pairs={{0,1},{1,2},{2,3},{3,0},{4,5},{5,6},{6,7},{7,4},{8,9},{9,10},{10,1... | collective-permute-start | bytes 192008 | tf_op jit(solution)/shard_map/ppermute | solution.py:306
  39.2 2.6 %collective-permute-start.1 = (f32[25,640]{1,0:T(8,128)}, f32[25,640]{1,0:T(8,128)S(1)}, u32[]{:S(2)}, u32[]{:S(2)}) collective-permute-start(f32[25,640]{1,0:T(8,128)} %get-tuple-element.13), channel_id=1, source_target_pairs={{0,2},{1,3},{2,0},{3,1},{4,6},{5,7},{6,4},{7,5},{8,10},{9,11},{10,... | collective-permute-start | bytes 192008 | tf_op jit(solution)/shard_map/ppermute | solution.py:306
  41.8 1.4 %collective-permute-start.2 = (f32[25,640]{1,0:T(8,128)}, f32[25,640]{1,0:T(8,128)S(1)}, u32[]{:S(2)}, u32[]{:S(2)}) collective-permute-start(f32[25,640]{1,0:T(8,128)} %get-tuple-element.14), channel_id=1, source_target_pairs={{0,3},{1,0},{2,1},{3,2},{4,7},{5,4},{6,5},{7,6},{8,11},{9,8},{10,9... | collective-permute-start | bytes 192008 | tf_op jit(solution)/shard_map/ppermute | solution.py:306
  43.1 0.6 broadcast_in_dim.14.home_ref
  43.7 0.6 broadcast_in_dim.13.assigned_ref
  44.3 0.4 collective-permute-done
  44.7 3.1 %collective-permute-done.1 = f32[25,640]{1,0:T(8,128)S(1)} collective-permute-done((f32[25,640]{1,0:T(8,128)}, f32[25,640]{1,0:T(8,128)S(1)}, u32[]{:S(2)}, u32[]{:S(2)}) %collective-permute-start.1) | collective-permute-done | bytes 64032 | tf_op jit(solution)/shard_map/ppermute | solution.py:306
  47.8 0.5 collective-permute-start.6
  48.4 2.2 %collective-permute-start.4 = (f32[3,48,300]{2,1,0:T(8,128)S(1)}, f32[3,48,300]{2,1,0:T(8,128)S(1)}, u32[]{:S(2)}, u32[]{:S(2)}) collective-permute-start(f32[3,48,300]{2,1,0:T(8,128)S(1)} %bitcast.14), channel_id=1, source_target_pairs={{0,8},{4,12},{8,16},{12,20},{16,24},{20,28},{24,0},{28,4},{1,9},{5... | collective-permute-start | bytes 518408 | tf_op jit(solution)/shard_map/ppermute | solution.py:306
  50.5 1.6 %multiply_reduce_fusion = (f32[640]{0:T(1024)S(1)}, f32[25,640]{1,0:T(8,128)}) fusion(f32[25,640]{1,0:T(8,128)S(1)} %collective-permute-done.2, f32[25,640]{1,0:T(8,128)S(1)} %collective-permute-done.1, f32[25,640]{1,0:T(8,128)} %get-tuple-element.11, f32[25,640]{1,0:T(8,128)S(1)} %collective-permute-done), kind=kLoop, calls=%fused_computation | loop fusion | flops 79360 | bytes 322560 | tf_op jit(solution)/shard_map/reduce_sum | solution.py:329
  52.2 2.8 %collective-permute-start.12 = (f32[1,640]{1,0:T(1,128)S(1)}, f32[1,640]{1,0:T(1,128)S(1)}, u32[]{:S(2)}, u32[]{:S(2)}) collective-permute-start(f32[1,640]{1,0:T(1,128)S(1)} %broadcast_in_dim.15.refs_0_), channel_id=1, source_target_pairs={{0,3},{1,0},{2,1},{3,2},{4,7},{5,4},{6,5},{7,6},{8,11},{9,8},{10,9... | collective-permute-start | bytes 7688 | tf_op jit(solution)/shard_map/ppermute | solution.py:306
  55.0 10.6 %collective-permute-done.6.refs_4_ = f32[3,48,300]{2,1,0:T(8,128)S(1)} collective-permute-done((f32[3,48,300]{2,1,0:T(8,128)S(1)}, f32[3,48,300]{2,1,0:T(8,128)S(1)}, u32[]{:S(2)}, u32[]{:S(2)}) %collective-permute-start.6) | collective-permute-done | bytes 172832 | tf_op jit(solution)/shard_map/ppermute | solution.py:306
  65.6 3.7 %collective-permute-start.11 = (f32[1,640]{1,0:T(1,128)S(1)}, f32[1,640]{1,0:T(1,128)S(1)}, u32[]{:S(2)}, u32[]{:S(2)}) collective-permute-start(f32[1,640]{1,0:T(1,128)S(1)} %broadcast_in_dim.15.refs_0_), channel_id=1, source_target_pairs={{0,2},{1,3},{2,0},{3,1},{4,6},{5,7},{6,4},{7,5},{8,10},{9,11},{10,... | collective-permute-start | bytes 7688 | tf_op jit(solution)/shard_map/ppermute | solution.py:306
  69.3 0.1 collective-permute-start.10
  69.5 0.5 copy-done.15
  70.0 0.2 copy-done.16
  70.2 0.7 copy-done.17
  70.9 6.1 %align.1 = (bf16[384,640]{1,0:T(8,128)(2,1)}, f32[240,640]{1,0:T(8,128)}) custom-call(f32[3,300,640]{2,1,0:T(8,128)} %bitcast.19, s32[1,640]{1,0:T(1,128)} %broadcast_in_dim.13.assigned_ref, s32[1,384]{1,0:T(1,128)} %broadcast_in_dim.14.home_ref, f32[3,48,300]{2,1,0:T(8,128)} %bitcast.9, f32[3,48,300]{2,1,0:T(8,128)} %copy-done.17, ...), custom_call_target="tpu_custom_call" | custom-call | flops 1769472000 | bytes 4194304 | tf_op jit(solution)/shard_map/align/pallas_call | solution.py:209
  77.0 0.5 copy-done.7
  77.6 0.0 copy-done.9
  77.6 2.5 %gather.1 = f32[8,48,256]{2,1,0:T(8,128)} custom-call(bf16[384,640]{1,0:T(8,128)(2,1)} %get-tuple-element.15.member_ref, f32[240,640]{1,0:T(8,128)} %get-tuple-element.16.aligned_ref, f32[1,640]{1,0:T(1,128)} %copy-done.5, f32[1,640]{1,0:T(1,128)} %copy-done.9, f32[1,640]{1,0:T(1,128)} %copy-done.8, f32[1,640]{1,0:T(1,128)} %copy-done.7), custom_call_target="tpu_custom_call" | custom-call | tf_op jit(solution)/shard_map/gather/pallas_call | solution.py:256
  80.1 11.7 %all_to_all.5 = f32[8,48,256]{2,1,0:T(8,128)S(1)} all-to-all(f32[8,48,256]{2,1,0:T(8,128)} %gather.1), channel_id=1, replica_groups=mesh['frames'=8,'pairs'=4] {'frames'}, dimensions={0} | all-to-all | bytes 786432 | tf_op jit(solution)/shard_map/all_to_all | solution.py:331
  91.8 3.7 %collective-permute-start.15 = (f32[48,256]{1,0:T(8,128)S(1)}, f32[48,256]{1,0:T(8,128)S(1)}, u32[]{:S(2)}, u32[]{:S(2)}) collective-permute-start(f32[48,256]{1,0:T(8,128)S(1)} %reduce_sum.19.refs_0_), channel_id=1, source_target_pairs={{0,3},{1,0},{2,1},{3,2},{4,7},{5,4},{6,5},{7,6},{8,11},{9,8},{10,9... | collective-permute-start | bytes 147464 | tf_op jit(solution)/shard_map/ppermute | solution.py:306
  95.6 0.6 collective-permute-start.13
  96.2 1.2 %collective-permute-done.15.refs_3_ = f32[48,256]{1,0:T(8,128)S(1)} collective-permute-done((f32[48,256]{1,0:T(8,128)S(1)}, f32[48,256]{1,0:T(8,128)S(1)}, u32[]{:S(2)}, u32[]{:S(2)}) %collective-permute-start.15) | collective-permute-done | bytes 49184 | tf_op jit(solution)/shard_map/ppermute | solution.py:306
  97.4 3.1 %collective-permute-done.14.refs_2_ = f32[48,256]{1,0:T(8,128)S(1)} collective-permute-done((f32[48,256]{1,0:T(8,128)S(1)}, f32[48,256]{1,0:T(8,128)S(1)}, u32[]{:S(2)}, u32[]{:S(2)}) %collective-permute-start.14) | collective-permute-done | bytes 49184 | tf_op jit(solution)/shard_map/ppermute | solution.py:306
  100.6 0.9 collective-permute-done.13.refs_1_
  101.5 0.6 copy-done.4
  102.1 1.9 %update.1 = (f32[3,48,300]{2,1,0:T(8,128)}, f32[1,48]{1,0:T(1,128)}) custom-call(f32[3,48,300]{2,1,0:T(8,128)} %bitcast.10, f32[48,256]{1,0:T(8,128)} %copy-done.1, f32[48,256]{1,0:T(8,128)} %copy-done.4, f32[48,256]{1,0:T(8,128)} %copy-done.3, f32[48,256]{1,0:T(8,128)} %copy-done.2), custom_call_target="tpu_custom_call" | custom-call | tf_op jit(solution)/shard_map/update/pallas_call | solution.py:292
  (46 shorter events, 0.1 us)
Async XLA Ops:
  0.6 47.7 %collective-permute-start.9 = (f32[3,48,300]{2,1,0:T(8,128)}, f32[3,48,300]{2,1,0:T(8,128)S(1)}, u32[]{:S(2)}, u32[]{:S(2)}) collective-permute-start(f32[3,48,300]{2,1,0:T(8,128)} %bitcast.7), channel_id=1, source_target_pairs={{0,28},{4,0},{8,4},{12,8},{16,12},{20,16},{24,20},{28,24},{1,29},{... | collective-permute-start | bytes 518408 | tf_op jit(solution)/shard_map/ppermute | solution.py:306
  4.0 46.5 %collective-permute-start.8 = (f32[3,48,300]{2,1,0:T(8,128)}, f32[3,48,300]{2,1,0:T(8,128)S(1)}, u32[]{:S(2)}, u32[]{:S(2)}) collective-permute-start(f32[3,48,300]{2,1,0:T(8,128)} %bitcast.8), channel_id=1, source_target_pairs={{0,24},{4,28},{8,0},{12,4},{16,8},{20,12},{24,16},{28,20},{1,25},{... | collective-permute-start | bytes 518408 | tf_op jit(solution)/shard_map/ppermute | solution.py:306
  4.6 38.5 %copy-start.10 = (s32[384]{0:T(512)S(1)}, s32[384]{0:T(512)}, u32[]{:S(2)}) copy-start(s32[384]{0:T(512)} %param.10) | copy-start | bytes 4612
  4.6 39.1 %copy-start.6 = (s32[640]{0:T(1024)S(1)}, s32[640]{0:T(1024)}, u32[]{:S(2)}) copy-start(s32[640]{0:T(1024)} %param.9) | copy-start | bytes 7684
  4.7 40.1 %copy-start = (f32[48,3,300]{2,0,1:T(8,128)S(1)}, f32[48,3,300]{2,0,1:T(8,128)}, u32[]{:S(2)}) copy-start(f32[48,3,300]{2,0,1:T(8,128)} %param.8) | copy-start | bytes 518404
  37.6 7.1 %collective-permute-start = (f32[25,640]{1,0:T(8,128)}, f32[25,640]{1,0:T(8,128)S(1)}, u32[]{:S(2)}, u32[]{:S(2)}) collective-permute-start(f32[25,640]{1,0:T(8,128)} %get-tuple-element.12), channel_id=1, source_target_pairs={{0,1},{1,2},{2,3},{3,0},{4,5},{5,6},{6,7},{7,4},{8,9},{9,10},{10,1... | collective-permute-start | bytes 192008 | tf_op jit(solution)/shard_map/ppermute | solution.py:306
  39.2 8.7 %collective-permute-start.1 = (f32[25,640]{1,0:T(8,128)}, f32[25,640]{1,0:T(8,128)S(1)}, u32[]{:S(2)}, u32[]{:S(2)}) collective-permute-start(f32[25,640]{1,0:T(8,128)} %get-tuple-element.13), channel_id=1, source_target_pairs={{0,2},{1,3},{2,0},{3,1},{4,6},{5,7},{6,4},{7,5},{8,10},{9,11},{10,... | collective-permute-start | bytes 192008 | tf_op jit(solution)/shard_map/ppermute | solution.py:306
  41.8 6.6 %collective-permute-start.2 = (f32[25,640]{1,0:T(8,128)}, f32[25,640]{1,0:T(8,128)S(1)}, u32[]{:S(2)}, u32[]{:S(2)}) collective-permute-start(f32[25,640]{1,0:T(8,128)} %get-tuple-element.14), channel_id=1, source_target_pairs={{0,3},{1,0},{2,1},{3,2},{4,7},{5,4},{6,5},{7,6},{8,11},{9,8},{10,9... | collective-permute-start | bytes 192008 | tf_op jit(solution)/shard_map/ppermute | solution.py:306
  44.7 7.4 %collective-permute-start.7 = (f32[3,48,300]{2,1,0:T(8,128)S(1)}, f32[3,48,300]{2,1,0:T(8,128)S(1)}, u32[]{:S(2)}, u32[]{:S(2)}) collective-permute-start(f32[3,48,300]{2,1,0:T(8,128)S(1)} %bitcast.11), channel_id=1, source_target_pairs={{0,20},{4,24},{8,28},{12,0},{16,4},{20,8},{24,12},{28,16},{1,21},{... | collective-permute-start | bytes 518408 | tf_op jit(solution)/shard_map/ppermute | solution.py:306
  47.8 17.8 %collective-permute-start.6 = (f32[3,48,300]{2,1,0:T(8,128)S(1)}, f32[3,48,300]{2,1,0:T(8,128)S(1)}, u32[]{:S(2)}, u32[]{:S(2)}) collective-permute-start(f32[3,48,300]{2,1,0:T(8,128)S(1)} %bitcast.12), channel_id=1, source_target_pairs={{0,16},{4,20},{8,24},{12,28},{16,0},{20,4},{24,8},{28,12},{1,17},{... | collective-permute-start | bytes 518408 | tf_op jit(solution)/shard_map/ppermute | solution.py:306
  48.3 21.0 %collective-permute-start.5 = (f32[3,48,300]{2,1,0:T(8,128)S(1)}, f32[3,48,300]{2,1,0:T(8,128)S(1)}, u32[]{:S(2)}, u32[]{:S(2)}) collective-permute-start(f32[3,48,300]{2,1,0:T(8,128)S(1)} %bitcast.13), channel_id=1, source_target_pairs={{0,12},{4,16},{8,20},{12,24},{16,28},{20,0},{24,4},{28,8},{1,13},{... | collective-permute-start | bytes 518408 | tf_op jit(solution)/shard_map/ppermute | solution.py:306
  48.3 21.2 %copy-start.11 = (f32[3,48,300]{2,1,0:T(8,128)}, f32[3,48,300]{2,1,0:T(8,128)S(1)}, u32[]{:S(2)}) copy-start(f32[3,48,300]{2,1,0:T(8,128)S(1)} %collective-permute-done.9.refs_7_) | copy-start | bytes 518404
  48.4 21.1 %collective-permute-start.4 = (f32[3,48,300]{2,1,0:T(8,128)S(1)}, f32[3,48,300]{2,1,0:T(8,128)S(1)}, u32[]{:S(2)}, u32[]{:S(2)}) collective-permute-start(f32[3,48,300]{2,1,0:T(8,128)S(1)} %bitcast.14), channel_id=1, source_target_pairs={{0,8},{4,12},{8,16},{12,20},{16,24},{20,28},{24,0},{28,4},{1,9},{5... | collective-permute-start | bytes 518408 | tf_op jit(solution)/shard_map/ppermute | solution.py:306
  50.5 19.0 %copy-start.12 = (f32[3,48,300]{2,1,0:T(8,128)}, f32[3,48,300]{2,1,0:T(8,128)S(1)}, u32[]{:S(2)}) copy-start(f32[3,48,300]{2,1,0:T(8,128)S(1)} %collective-permute-done.8.refs_6_) | copy-start | bytes 518404
  50.5 19.0 %collective-permute-start.3 = (f32[3,48,300]{2,1,0:T(8,128)S(1)}, f32[3,48,300]{2,1,0:T(8,128)S(1)}, u32[]{:S(2)}, u32[]{:S(2)}) collective-permute-start(f32[3,48,300]{2,1,0:T(8,128)S(1)} %bitcast.15), channel_id=1, source_target_pairs={{0,4},{4,8},{8,12},{12,16},{16,20},{20,24},{24,28},{28,0},{1,5},{5... | collective-permute-start | bytes 518408 | tf_op jit(solution)/shard_map/ppermute | solution.py:306
  52.2 24.8 %copy-start.5 = (f32[1,640]{1,0:T(1,128)}, f32[1,640]{1,0:T(1,128)S(1)}, u32[]{:S(2)}) copy-start(f32[1,640]{1,0:T(1,128)S(1)} %broadcast_in_dim.15.refs_0_) | copy-start | bytes 7684
  52.2 17.3 %copy-start.13 = (f32[3,48,300]{2,1,0:T(8,128)}, f32[3,48,300]{2,1,0:T(8,128)S(1)}, u32[]{:S(2)}) copy-start(f32[3,48,300]{2,1,0:T(8,128)S(1)} %collective-permute-done.7.refs_5_) | copy-start | bytes 518404
  52.2 24.8 %collective-permute-start.12 = (f32[1,640]{1,0:T(1,128)S(1)}, f32[1,640]{1,0:T(1,128)S(1)}, u32[]{:S(2)}, u32[]{:S(2)}) collective-permute-start(f32[1,640]{1,0:T(1,128)S(1)} %broadcast_in_dim.15.refs_0_), channel_id=1, source_target_pairs={{0,3},{1,0},{2,1},{3,2},{4,7},{5,4},{6,5},{7,6},{8,11},{9,8},{10,9... | collective-permute-start | bytes 7688 | tf_op jit(solution)/shard_map/ppermute | solution.py:306
  65.6 3.9 %copy-start.14 = (f32[3,48,300]{2,1,0:T(8,128)}, f32[3,48,300]{2,1,0:T(8,128)S(1)}, u32[]{:S(2)}) copy-start(f32[3,48,300]{2,1,0:T(8,128)S(1)} %collective-permute-done.6.refs_4_) | copy-start | bytes 518404
  65.6 11.4 %collective-permute-start.11 = (f32[1,640]{1,0:T(1,128)S(1)}, f32[1,640]{1,0:T(1,128)S(1)}, u32[]{:S(2)}, u32[]{:S(2)}) collective-permute-start(f32[1,640]{1,0:T(1,128)S(1)} %broadcast_in_dim.15.refs_0_), channel_id=1, source_target_pairs={{0,2},{1,3},{2,0},{3,1},{4,6},{5,7},{6,4},{7,5},{8,10},{9,11},{10,... | collective-permute-start | bytes 7688 | tf_op jit(solution)/shard_map/ppermute | solution.py:306
  69.3 0.7 copy-start.15
  69.3 7.7 %collective-permute-start.10 = (f32[1,640]{1,0:T(1,128)S(1)}, f32[1,640]{1,0:T(1,128)S(1)}, u32[]{:S(2)}, u32[]{:S(2)}) collective-permute-start(f32[1,640]{1,0:T(1,128)S(1)} %broadcast_in_dim.15.refs_0_), channel_id=1, source_target_pairs={{0,1},{1,2},{2,3},{3,0},{4,5},{5,6},{6,7},{7,4},{8,9},{9,10},{10,1... | collective-permute-start | bytes 7688 | tf_op jit(solution)/shard_map/ppermute | solution.py:306
  69.5 0.7 copy-start.16
  70.2 0.7 copy-start.17
  77.0 0.6 copy-start.7
  91.8 9.6 %copy-start.1 = (f32[48,256]{1,0:T(8,128)}, f32[48,256]{1,0:T(8,128)S(1)}, u32[]{:S(2)}) copy-start(f32[48,256]{1,0:T(8,128)S(1)} %reduce_sum.19.refs_0_) | copy-start | bytes 147460
  91.8 5.6 %collective-permute-start.15 = (f32[48,256]{1,0:T(8,128)S(1)}, f32[48,256]{1,0:T(8,128)S(1)}, u32[]{:S(2)}, u32[]{:S(2)}) collective-permute-start(f32[48,256]{1,0:T(8,128)S(1)} %reduce_sum.19.refs_0_), channel_id=1, source_target_pairs={{0,3},{1,0},{2,1},{3,2},{4,7},{5,4},{6,5},{7,6},{8,11},{9,8},{10,9... | collective-permute-start | bytes 147464 | tf_op jit(solution)/shard_map/ppermute | solution.py:306
  95.6 5.0 %collective-permute-start.14 = (f32[48,256]{1,0:T(8,128)S(1)}, f32[48,256]{1,0:T(8,128)S(1)}, u32[]{:S(2)}, u32[]{:S(2)}) collective-permute-start(f32[48,256]{1,0:T(8,128)S(1)} %reduce_sum.19.refs_0_), channel_id=1, source_target_pairs={{0,2},{1,3},{2,0},{3,1},{4,6},{5,7},{6,4},{7,5},{8,10},{9,11},{10,... | collective-permute-start | bytes 147464 | tf_op jit(solution)/shard_map/ppermute | solution.py:306
  95.6 5.9 %collective-permute-start.13 = (f32[48,256]{1,0:T(8,128)S(1)}, f32[48,256]{1,0:T(8,128)S(1)}, u32[]{:S(2)}, u32[]{:S(2)}) collective-permute-start(f32[48,256]{1,0:T(8,128)S(1)} %reduce_sum.19.refs_0_), channel_id=1, source_target_pairs={{0,1},{1,2},{2,3},{3,0},{4,5},{5,6},{6,7},{7,4},{8,9},{9,10},{10,1... | collective-permute-start | bytes 147464 | tf_op jit(solution)/shard_map/ppermute | solution.py:306
  97.4 4.0 %copy-start.2 = (f32[48,256]{1,0:T(8,128)}, f32[48,256]{1,0:T(8,128)S(1)}, u32[]{:S(2)}) copy-start(f32[48,256]{1,0:T(8,128)S(1)} %collective-permute-done.15.refs_3_) | copy-start | bytes 147460
  100.5 0.9 copy-start.3
  101.5 0.6 copy-start.4
  (2 other events, 1.2 us)

commit v2 on v1

--- a/solution.py
+++ b/solution.py
@@ -9,7 +9,7 @@
 
 NEWTON = 8
 PIECES = 3
-VMEM_BYTES = 60 * 2**20
+MIB = 2**20
 
 prior_weight = 4.0
 piece_type = jnp.float8_e4m3fn
@@ -23,48 +23,99 @@
     return rows - jnp.sum(rows, axis=0, keepdims=True) / rows.shape[0]
 
 
-def load_pieces(coords_ref, split_ref, positions_ref, unit_ref, stride):
+LANES = 128
+DEPTH = 8 * LANES
+HALF = LANES // 2
+REACH = 247.0
+
+
+def tail_lanes(res_count):
+    tail = res_count - 2 * LANES
+    assert 0 < tail <= HALF
+    return tail
+
+
+def split_kernel(coords_ref, positions_ref, unit_ref, rows_ref):
     dims, res_count, frames = coords_ref.shape
+    tail = tail_lanes(res_count)
     centered = [center_rows(coords_ref[c]) for c in range(dims)]
     reach = functools.reduce(
         jnp.maximum, [jnp.max(jnp.abs(rows), axis=0, keepdims=True) for rows in centered]
     )
     reach = jnp.maximum(reach, 1e-30)
-    unit_ref[...] = jnp.broadcast_to(reach * (1.0 / 256.0), (128, frames)).T
-    scale = 256.0 / reach
-    split_ref[...] = jnp.zeros_like(split_ref)
+    unit_ref[...] = jnp.broadcast_to(reach * (1.0 / REACH), (128, frames)).T
+    scale = REACH / reach
+    rows_ref[res_count:, :] = jnp.zeros((rows_ref.shape[0] - res_count, frames), jnp.float32)
+    lane = lax.broadcasted_iota(jnp.int32, (frames, LANES), 1)
     for c in range(dims):
-        rest = centered[c] * scale
-        for k in range(PIECES):
-            piece = rest.astype(piece_type).astype(jnp.float32)
-            split_ref[k * stride : k * stride + res_count, :] = piece
-            rest = rest - piece
-        positions_ref[c * frames : (c + 1) * frames, :] = split_ref[...].T.astype(piece_type)
+        rows_ref[0:res_count, :] = centered[c] * scale
+        rest = rows_ref[...].T
+        pieces = []
+        for k in range(PIECES - 1):
+            shift = 1.5 * 2.0**23 * 16.0 / 32.0**k
+            pieces.append((rest + shift) - shift)
+            rest = rest - pieces[-1]
+        pieces.append(rest)
+        high, mid, low = [
+            [piece[:, g * LANES : (g + 1) * LANES] for g in range(3)] for piece in pieces
+        ]
+        mixed = jnp.where(lane < tail, high[2], mid[1])
+        shared = jnp.concatenate([mid[1][:, 0:HALF], mid[2][:, 0:HALF]], axis=1)
+        groups = [high[0], high[1], mixed, mid[0], low[0], low[1], low[2], shared]
+        for g, group in enumerate(groups):
+            positions_ref[c * frames : (c + 1) * frames, g * LANES : (g + 1) * LANES] = group.astype(
+                piece_type
+            )
+
+
+def split_coords(coords):
+    dims, res_count, frames = coords.shape
+    return pl.pallas_call(
+        split_kernel,
+        out_shape=[
+            jax.ShapeDtypeStruct((dims * frames, DEPTH), piece_type),
+            jax.ShapeDtypeStruct((frames, 128), jnp.float32),
+        ],
+        scratch_shapes=[pltpu.VMEM((round_up(res_count, 128), frames), jnp.float32)],
+        compiler_params=pltpu.CompilerParams(vmem_limit_bytes=24 * MIB),
+        cost_estimate=pl.CostEstimate(
+            flops=2**30, bytes_accessed=2**23, transcendentals=0
+        ),
+        name="split",
+    )(coords)
 
 
 def project_kernel(
-    axis, share, index_ref, mean_ref, weight_ref, coords_ref, *refs
+    axis, share, res_count, index_ref, mean_ref, weight_ref, positions_ref, unit_ref, *refs
 ):
-    out_refs = refs[:-5]
-    split_ref, positions_ref, unit_ref, selector_ref, total_ref = refs[-5:]
-    dims, res_count, frames = coords_ref.shape
+    out_refs = refs[:-2]
+    selector_ref, total_ref = refs[-2:]
     comps, pairs = weight_ref.shape
+    frames = unit_ref.shape[0]
+    dims = positions_ref.shape[0] // frames
+    tail = tail_lanes(res_count)
     step = pl.program_id(0)
-    stride = round_up(res_count, 32)
 
     @pl.when(step == 0)
     def _():
-        load_pieces(coords_ref, split_ref, positions_ref, unit_ref, stride)
         total_ref[...] = jnp.zeros_like(total_ref)
-        selector_ref[...] = jnp.zeros_like(selector_ref)
-
-    residue = lax.broadcasted_iota(jnp.int32, (stride, pairs), 0)
-    selector = (
-        jnp.where(residue == index_ref[0:1, :], 1.0, 0.0)
-        - jnp.where(residue == index_ref[1:2, :], 1.0, 0.0)
-    ).astype(piece_type)
-    for k in range(PIECES):
-        selector_ref[k * stride : (k + 1) * stride, :] = selector
+
+    def select(residue):
+        return (
+            jnp.where(residue == index_ref[0:1, :], 1.0, 0.0)
+            - jnp.where(residue == index_ref[1:2, :], 1.0, 0.0)
+        ).astype(piece_type)
+
+    line = lax.broadcasted_iota(jnp.int32, (LANES, pairs), 0)
+    firsts, lasts = select(line), select(line + 2 * LANES)
+    middle = select(line + LANES)
+    shared = select(
+        jnp.where(line < HALF, jnp.where(line < tail, line + LANES, -1), line + 2 * LANES - HALF)
+    )
+    mixed = select(jnp.where(line < tail, line + 2 * LANES, line + LANES))
+    groups = [firsts, middle, mixed, firsts, firsts, middle, lasts, shared]
+    for g, group in enumerate(groups):
+        selector_ref[g * LANES : (g + 1) * LANES, :] = group
     square = None
     for c in range(dims):
         diff = jnp.dot(
@@ -89,44 +140,43 @@
         rows = [flipped[k * share : (k + 1) * share, :] for k in range(parts)]
         me = lax.axis_index(axis)
         for s, out_ref in enumerate(out_refs):
-            owner = lax.rem(me + s, parts)
             value = rows[0]
             for k in range(1, parts):
-                value = jnp.where(owner == k, rows[k], value)
+                value = jnp.where(me ^ s == k, rows[k], value)
             out_ref[...] = value
 
 
-def project(coords, pair_index, mean_dist, tica_weight, axis):
-    dims, res_count, frames = coords.shape
+def project(positions, unit, res_count, pair_index, mean_dist, tica_weight, axis):
+    frames = unit.shape[0]
     comps, pairs = tica_weight.shape
     parts = lax.axis_size(axis)
     share = comps // parts
     block = next(b for b in (2816, 1408, 1024, 512, 256, 128, pairs) if pairs % b == 0)
-    depth = round_up(PIECES * round_up(res_count, 32), 256)
-    return pl.pallas_call(
-        functools.partial(project_kernel, axis, share),
+    depth = positions.shape[1]
+    return pl.pallas_call(
+        functools.partial(project_kernel, axis, share, res_count),
         grid=(pairs // block,),
         in_specs=[
             pl.BlockSpec((2, block), lambda i: (0, i)),
             pl.BlockSpec((1, block), lambda i: (0, i)),
             pl.BlockSpec((comps, block), lambda i: (0, i)),
-            pl.BlockSpec((dims, res_count, frames), lambda i: (0, 0, 0)),
+            pl.BlockSpec(positions.shape, lambda i: (0, 0)),
+            pl.BlockSpec(unit.shape, lambda i: (0, 0)),
         ],
         out_specs=[pl.BlockSpec((share, frames), lambda i: (0, 0))] * parts,
         out_shape=[jax.ShapeDtypeStruct((share, frames), jnp.float32)] * parts,
         scratch_shapes=[
-            pltpu.VMEM((depth, frames), jnp.float32),
-            pltpu.VMEM((dims * frames, depth), piece_type),
-            pltpu.VMEM((frames, 128), jnp.float32),
             pltpu.VMEM((depth, block), piece_type),
             pltpu.VMEM((frames, round_up(comps, 128)), jnp.float32),
         ],
-        compiler_params=pltpu.CompilerParams(vmem_limit_bytes=VMEM_BYTES),
+        compiler_params=pltpu.CompilerParams(vmem_limit_bytes=48 * MIB),
         cost_estimate=pl.CostEstimate(
-            flops=2 * dims * frames * pairs * depth, bytes_accessed=8 * 2**20, transcendentals=0
+            flops=2 * positions.shape[0] * pairs * depth,
+            bytes_accessed=8 * 2**20,
+            transcendentals=0,
         ),
         name="project",
-    )(pair_index, mean_dist, tica_weight, coords)
+    )(pair_index, mean_dist, tica_weight, positions, unit)
 
 
 def polar_factor(cross):
@@ -159,17 +209,18 @@
     piece_refs = refs[:parts]
     member_ref, aligned_ref, refs_ref, centered_ref = refs[parts:]
     dims, res_count, frames = coords_ref.shape
-    micro = home_ref.shape[1]
-    local_micro = piece_refs[0].shape[1]
+    micro = home_ref.shape[0]
+    both, local_micro = piece_refs[0].shape[0], piece_refs[0].shape[2]
     me = lax.axis_index(frames_axis)
     for s, piece_ref in enumerate(piece_refs):
-        owner = lax.rem(me + parts - s, parts)
-        at = pl.multiple_of(owner * local_micro, 8)
-        refs_ref[:, pl.ds(at, local_micro), :] = piece_ref[...]
+        for k in range(both):
+            owner = me ^ (both * s + k)
+            at = pl.multiple_of(owner * local_micro, 8)
+            refs_ref[:, pl.ds(at, local_micro), :] = piece_ref[k]
 
     state = lax.broadcasted_iota(jnp.int32, (micro, frames), 0)
-    chosen = (state == assigned_ref[...]).astype(jnp.float32).astype(jnp.bfloat16)
-    home = home_ref[...]
+    chosen = (state == assigned_ref[...].reshape(1, frames)).astype(jnp.float32).astype(jnp.bfloat16)
+    home = home_ref[...].reshape(1, micro)
     half = lax.broadcasted_iota(jnp.int32, (16, micro), 0)
     halves = jnp.where(half == 0, home >> 5, jnp.where(half == 1, home & 31, 0))
     picked = jnp.dot(
@@ -204,7 +255,7 @@
 
 def align(coords, assignment, home_row, pieces, frames_axis, pairs_axis, quarter):
     dims, res_count, frames = coords.shape
-    micro = home_row.shape[1]
+    micro = home_row.shape[0]
     whole = quarter * lax.axis_size(pairs_axis)
     return pl.pallas_call(
         functools.partial(align_kernel, frames_axis, pairs_axis, quarter),
@@ -216,7 +267,7 @@
             pltpu.VMEM((dims, micro, res_count), jnp.float32),
             pltpu.VMEM((dims, whole, frames), jnp.float32),
         ],
-        compiler_params=pltpu.CompilerParams(vmem_limit_bytes=VMEM_BYTES),
+        compiler_params=pltpu.CompilerParams(vmem_limit_bytes=40 * MIB),
         cost_estimate=pl.CostEstimate(
             flops=8 * dims * frames * micro * res_count, bytes_accessed=2**22, transcendentals=0
         ),
@@ -224,13 +275,12 @@
     )(coords, assignment, home_row, *pieces)
 
 
-def gather_kernel(axis, comps, member_ref, aligned_ref, *refs):
-    square_refs = refs[:-3]
-    out_ref, square_ref, weighted_ref = refs[-3:]
-    parts = len(square_refs)
+def gather_kernel(axis, owners_axis, comps, parts, member_ref, aligned_ref, *refs):
+    square_refs = refs[:parts]
+    out_refs, (square_ref, weighted_ref, summed_ref) = refs[parts:-3], refs[-3:]
     me = lax.axis_index(axis)
     for s, ref in enumerate(square_refs):
-        square_ref[lax.rem(me + parts - s, parts)] = ref[...]
+        square_ref[me ^ s] = ref[...]
     square = sum(square_ref[k] for k in range(parts))
     weight = 1.0 / (1.0 + 4.0 * (square / comps))
     rows = aligned_ref.shape[0]
@@ -243,26 +293,48 @@
     low = (weighted - high.astype(jnp.float32)).astype(jnp.bfloat16)
     member = member_ref[...]
     over_frames = (((1,), (1,)), ((), ()))
-    summed = lax.dot_general(
+    summed_ref[...] = lax.dot_general(
         member, high, over_frames, preferred_element_type=jnp.float32
     ) + lax.dot_general(member, low, over_frames, preferred_element_type=jnp.float32)
-    out_ref[...] = summed.reshape(out_ref.shape)
-
-
-def gather(member, aligned, squares, axis, comps, owners):
+    here = lax.axis_index(owners_axis)
+    for k, out_ref in enumerate(out_refs):
+        states = out_ref.shape[1]
+        for s in range(out_ref.shape[0]):
+            at = pl.multiple_of((here ^ (2 * s + k)) * states, 8)
+            out_ref[s] = summed_ref[pl.ds(at, states), :]
+
+
+def gather(member, aligned, squares, axis, owners_axis, comps):
     micro, frames = member.shape
+    owners = lax.axis_size(owners_axis)
     rows = aligned.shape[0]
     width = round_up(rows + 1, 128)
     return pl.pallas_call(
-        functools.partial(gather_kernel, axis, comps),
-        out_shape=jax.ShapeDtypeStruct((owners, micro // owners, width), jnp.float32),
+        functools.partial(gather_kernel, axis, owners_axis, comps, len(squares)),
+        out_shape=[jax.ShapeDtypeStruct((owners // 2, micro // owners, width), jnp.float32)] * 2,
         scratch_shapes=[
             pltpu.VMEM((len(squares), 1, frames), jnp.float32),
             pltpu.VMEM((width, frames), jnp.float32),
-        ],
-        compiler_params=pltpu.CompilerParams(vmem_limit_bytes=VMEM_BYTES),
+            pltpu.VMEM((micro, width), jnp.float32),
+        ],
+        compiler_params=pltpu.CompilerParams(vmem_limit_bytes=16 * MIB),
         name="gather",
     )(member, aligned, *squares)
+
+
+def merge_kernel(mine_ref, other_ref, *out_refs):
+    for s, out_ref in enumerate(out_refs):
+        out_ref[...] = mine_ref[s] + other_ref[s]
+
+
+def merge(mine, other):
+    count = mine.shape[0]
+    return pl.pallas_call(
+        merge_kernel,
+        out_shape=[jax.ShapeDtypeStruct(mine.shape[1:], jnp.float32)] * count,
+        compiler_params=pltpu.CompilerParams(vmem_limit_bytes=8 * MIB),
+        name="merge",
+    )(mine, other)
 
 
 def update_kernel(axis, quarter, centroids_ref, *refs):
@@ -272,7 +344,7 @@
     dims, states, res_count = centroids_ref.shape
     me = lax.axis_index(axis)
     for s, ref in enumerate(piece_refs):
-        pieces_ref[lax.rem(me + parts - s, parts)] = ref[...]
+        pieces_ref[me ^ s] = ref[...]
     occupancy = pieces_ref[0][:, dims * quarter : dims * quarter + 1]
     row = lax.broadcasted_iota(jnp.int32, (states, states), 0)
     column = lax.broadcasted_iota(jnp.int32, (states, states), 1)
@@ -296,41 +368,53 @@
             jax.ShapeDtypeStruct((1, states), jnp.float32),
         ],
         scratch_shapes=[pltpu.VMEM((len(pieces),) + pieces[0].shape, jnp.float32)],
-        compiler_params=pltpu.CompilerParams(vmem_limit_bytes=VMEM_BYTES),
+        compiler_params=pltpu.CompilerParams(vmem_limit_bytes=8 * MIB),
         name="update",
     )(centroids, *pieces)
 
 
-def from_behind(value, axis, step):
+def swap(value, axis, step):
     size = lax.axis_size(axis)
-    return lax.ppermute(value, axis, [(i, (i + step) % size) for i in range(size)])
-
-
-def gathered(value, axis):
-    return [value] + [from_behind(value, axis, s) for s in range(1, lax.axis_size(axis))]
+    return lax.ppermute(value, axis, [(i, i ^ step) for i in range(size)])
+
+
+def gathered(value, axis, first=1):
+    steps = range(first, lax.axis_size(axis), first)
+    return [value] + [swap(value, axis, s) for s in steps]
 
 
 def local(coords, centroids, assignment, home_row, pair_index, mean_dist, tica_weight):
     comps = tica_weight.shape[1]
     parts = lax.axis_size("pairs")
-    owners = lax.axis_size("frames")
     coords = jnp.transpose(coords, (1, 2, 0))
     centroids = jnp.transpose(centroids, (1, 0, 2))
     quarter = round_up(-(-coords.shape[1] // parts), 8)
 
-    refs = gathered(centroids, "frames")
-    partial = project(coords, pair_index, mean_dist[None, :], tica_weight.T, "pairs")
+    other = swap(centroids, "frames", 1)
+    positions, unit = split_coords(coords)
+    positions, both = lax.optimization_barrier((positions, jnp.stack([centroids, other])))
+    refs = gathered(both, "frames", 2)
+    partial = project(
+        positions, unit, coords.shape[1], pair_index, mean_dist[None, :], tica_weight.T, "pairs"
+    )
+    partial, refs = lax.optimization_barrier((partial, refs))
+    received = [swap(partial[s], "pairs", s) for s in range(1, parts)]
+    member, aligned, received = lax.optimization_barrier(
+        (
+            *align(coords, assignment, home_row, refs, "frames", "pairs", quarter),
+            received,
+        )
+    )
     tica = partial[0]
-    for s in range(1, parts):
-        tica = tica + from_behind(partial[s], "pairs", s)
-    member, aligned = align(
-        coords, assignment[None, :], home_row[None, :], refs, "frames", "pairs", quarter
-    )
+    for piece in received:
+        tica = tica + piece
     squares = gathered(jnp.sum(tica * tica, axis=0, keepdims=True), "pairs")
-    sums = gather(member, aligned, squares, "pairs", comps, owners)
-    sums = lax.all_to_all(sums, "frames", split_axis=0, concat_axis=0, tiled=True)
-    sums = jnp.sum(sums, axis=0)
-    new_centroids, occupancy = update(centroids, gathered(sums, "pairs"), "pairs", quarter)
+    mine, other = gather(member, aligned, squares, "pairs", "frames", comps)
+    sums = merge(mine, swap(other, "frames", 1))
+    total = sums[0]
+    for s in range(1, len(sums)):
+        total = total + swap(sums[s], "frames", 2 * s)
+    new_centroids, occupancy = update(centroids, gathered(total, "pairs"), "pairs", quarter)
     return (tica.T, jnp.transpose(new_centroids, (1, 0, 2)), occupancy[0])
 
 

time: 104 us -> 74.1 us (0.71)
  blocking collectives: 11.7 us -> 0 us
  Pallas kernels: 43.5 us -> 34 us
  waiting for transfers between devices: 19.4 us -> 14.9 us
  local copies, waits for them, and re-layouts: 3.76 us -> 1.69 us
  starting transfers between devices: 23.3 us -> 21.8 us
    all_to_all x1 -> x0, blocking collectives: 11.7 us -> none  [local(): lax.all_to_all(sums, 'frames', split_axis=0, concat_axis=0, tiled=True)]
    pallas_call x2 -> x4, Pallas kernels: 35.4 us -> 30 us  [the longest x1 27.8 us: project(): pl.pallas_call(functools.partial(project_kernel, axis, share, res_count),...]
    ppermute x16 -> x17, waiting for transfers between devices: 19.4 us -> 14.9 us  [swap(): return lax.ppermute(value, axis, [(i, i ^ step) for i in range(size)])]
    pallas_call x1, Pallas kernels: 6.07 us -> 3.09 us  [align(): pl.pallas_call(functools.partial(align_kernel, frames_axis, pairs_axis, q...]
    ppermute x16 -> x17, starting transfers between devices: 23.3 us -> 21.8 us  [swap(): return lax.ppermute(value, axis, [(i, i ^ step) for i in range(size)])]
    broadcast_in_dim x2 -> x0, local copies, waits for them, and re-layouts: 1.18 us -> none  [the longest x1 0.59 us: local(): home_row[None, :]]
    unnamed x36 -> x16, local copies, waits for them, and re-layouts: 2.57 us -> 1.69 us
  transfers between devices with their start and end apart: 16 -> 17, of which waited for: 6 -> 9; matrix products, arithmetic and copies ran while one was open for 3% -> 0% of each run, Pallas kernels for 38% -> 44%
where the time goes in v2:
time: 74.1 us; the launch traced here: 73.9 us
  Pallas kernels  34 us (46%)
  starting transfers between devices  21.8 us (29%)
  waiting for transfers between devices  14.9 us (20%)
  local copies, waits for them, and re-layouts  1.69 us (2%)
  between operations  0.79 us (1%)
    pallas_call x1, Pallas kernels, project(): pl.pallas_call(functools.partial(project_kernel, axis, share, res_count),...  27.8 us
    ppermute x17, starting transfers between devices, swap(): return lax.ppermute(value, axis, [(i, i ^ step) for i in range(size)])  21.8 us
    ppermute x17, waiting for transfers between devices, swap(): return lax.ppermute(value, axis, [(i, i ^ step) for i in range(size)])  14.9 us
    pallas_call x1, Pallas kernels, align(): pl.pallas_call(functools.partial(align_kernel, frames_axis, pairs_axis, q...  3.09 us
    unnamed x16, local copies, waits for them, and re-layouts  1.69 us
    pallas_call x1, Pallas kernels, split_coords(): pl.pallas_call(split_kernel, out_shape=[jax.ShapeDtypeStruct((dims * fram...  1.55 us
  transfers between devices with their start and end apart: 17, of which 9 were waited for; matrix products, arithmetic and copies ran while one was open for 0% of the time, Pallas kernels for 44%

profile of v2, /device:TPU:0, one launch (start us, length us, event | category | flops | bytes accessed | tf_op | source)
XLA Modules:
  0.0 73.9 jit_solution(8480909540449445647)
XLA Ops:
  0.6 0.5 collective-permute-start
  1.2 1.7 %copy-done.2 = f32[640,3,300]{0,2,1:T(8,128)S(1)} copy-done((f32[640,3,300]{0,2,1:T(8,128)S(1)}, f32[640,3,300]{0,2,1:T(8,128)}, u32[]{:S(2)}) %copy-start.2) | copy-done | bytes 2304024
  2.8 1.6 %split.1 = (f8e4m3fn[1920,1024]{1,0:T(32,128)(4,1)S(1)}, f32[640,128]{1,0:T(8,128)S(1)}) custom-call(f32[3,300,640]{2,1,0:T(8,128)S(1)} %bitcast.14), custom_call_target="tpu_custom_call" | custom-call | flops 1073741824 | bytes 8388608 | tf_op jit(solution)/shard_map/split/pallas_call | solution.py:73
  4.4 3.6 %collective-permute-start.3 = (f32[2,3,48,300]{3,2,1,0:T(8,128)S(1)}, f32[2,3,48,300]{3,2,1,0:T(8,128)S(1)}, u32[]{:S(2)}, u32[]{:S(2)}) collective-permute-start(f32[2,3,48,300]{3,2,1,0:T(8,128)S(1)} %pad_maximum_fusion.refs_0_), channel_id=1, source_target_pairs={{0,24},{4,28},{8,16},{12,20},{16,8},{20,12},{24,0},{28,4},{1,25},{... | collective-permute-start | bytes 1036808 | tf_op jit(solution)/shard_map/ppermute | solution.py:378
  8.0 0.5 collective-permute-start.2
  8.5 0.1 collective-permute-start.1
  8.7 27.8 %project.1 = (f32[25,640]{1,0:T(8,128)S(1)}, f32[25,640]{1,0:T(8,128)S(1)}, f32[25,640]{1,0:T(8,128)S(1)}, f32[25,640]{1,0:T(8,128)S(1)}) custom-call(s32[2,11264]{1,0:T(2,128)S(1)} %copy-done.4, f32[1,11264]{1,0:T(1,128)S(1)} %bitcast.16, bf16[100,11264]{1,0:T(8,128)(2,1)S(1)} %bitcast.13, f8e4m3fn[1920,1024]{1,0:T(32,128)(4,1)S(1)} %get-tuple-element.35.positions_ref, ...), custom_call_target="tpu_custom_call" | custom-call | flops 44291850240 | bytes 8388608 | tf_op jit(solution)/shard_map/project/pallas_call | solution.py:156
  36.6 2.0 %collective-permute-start.4 = (f32[25,640]{1,0:T(8,128)S(1)}, f32[25,640]{1,0:T(8,128)S(1)}, u32[]{:S(2)}, u32[]{:S(2)}) collective-permute-start(f32[25,640]{1,0:T(8,128)S(1)} %get-tuple-element.49), channel_id=1, source_target_pairs={{0,1},{1,0},{2,3},{3,2},{4,5},{5,4},{6,7},{7,6},{8,9},{9,8},{10,11... | collective-permute-start | bytes 192008 | tf_op jit(solution)/shard_map/ppermute | solution.py:378
  38.6 2.6 %collective-permute-start.5 = (f32[25,640]{1,0:T(8,128)S(1)}, f32[25,640]{1,0:T(8,128)S(1)}, u32[]{:S(2)}, u32[]{:S(2)}) collective-permute-start(f32[25,640]{1,0:T(8,128)S(1)} %get-tuple-element.50), channel_id=1, source_target_pairs={{0,2},{1,3},{2,0},{3,1},{4,6},{5,7},{6,4},{7,5},{8,10},{9,11},{10,... | collective-permute-start | bytes 192008 | tf_op jit(solution)/shard_map/ppermute | solution.py:378
  41.2 3.1 %align.1 = (bf16[384,640]{1,0:T(8,128)(2,1)S(1)}, f32[240,640]{1,0:T(8,128)S(1)}) custom-call(f32[3,300,640]{2,1,0:T(8,128)S(1)} %bitcast.15, s32[640]{0:T(1024)S(1)} %copy-done.6, s32[384]{0:T(512)S(1)} %copy-done.7, f32[2,3,48,300]{3,2,1,0:T(8,128)S(1)} %pad_maximum_fusion.refs_0_, f32[2,3,48,300]{3,2,1,0:T(8,128)S(1)} %collective-permute-done.1.refs_1_, ...), custom_call_target="tpu_custom_call" | custom-call | flops 1769472000 | bytes 4194304 | tf_op jit(solution)/shard_map/align/pallas_call | solution.py:260
  44.3 3.3 %collective-permute-done.5 = f32[25,640]{1,0:T(8,128)S(1)} collective-permute-done((f32[25,640]{1,0:T(8,128)S(1)}, f32[25,640]{1,0:T(8,128)S(1)}, u32[]{:S(2)}, u32[]{:S(2)}) %collective-permute-start.5) | collective-permute-done | bytes 64032 | tf_op jit(solution)/shard_map/ppermute | solution.py:378
  47.6 0.7 multiply_reduce_fusion
  48.3 2.5 %collective-permute-start.9 = (f32[1,640]{1,0:T(1,128)S(1)}, f32[1,640]{1,0:T(1,128)S(1)}, u32[]{:S(2)}, u32[]{:S(2)}) collective-permute-start(f32[1,640]{1,0:T(1,128)S(1)} %broadcast_in_dim.7.refs_0_), channel_id=1, source_target_pairs={{0,3},{1,2},{2,1},{3,0},{4,7},{5,6},{6,5},{7,4},{8,11},{9,10},{10,... | collective-permute-start | bytes 7688 | tf_op jit(solution)/shard_map/ppermute | solution.py:378
  50.7 0.4 collective-permute-start.8
  51.2 1.5 %collective-permute-start.7 = (f32[1,640]{1,0:T(1,128)S(1)}, f32[1,640]{1,0:T(1,128)S(1)}, u32[]{:S(2)}, u32[]{:S(2)}) collective-permute-start(f32[1,640]{1,0:T(1,128)S(1)} %broadcast_in_dim.7.refs_0_), channel_id=1, source_target_pairs={{0,1},{1,0},{2,3},{3,2},{4,5},{5,4},{6,7},{7,6},{8,9},{9,8},{10,11... | collective-permute-start | bytes 7688 | tf_op jit(solution)/shard_map/ppermute | solution.py:378
  52.6 1.0 %collective-permute-done.9.refs_3_ = f32[1,640]{1,0:T(1,128)S(1)} collective-permute-done((f32[1,640]{1,0:T(1,128)S(1)}, f32[1,640]{1,0:T(1,128)S(1)}, u32[]{:S(2)}, u32[]{:S(2)}) %collective-permute-start.9) | collective-permute-done | bytes 2592 | tf_op jit(solution)/shard_map/ppermute | solution.py:378
  53.6 1.6 %collective-permute-done.8.refs_2_ = f32[1,640]{1,0:T(1,128)S(1)} collective-permute-done((f32[1,640]{1,0:T(1,128)S(1)}, f32[1,640]{1,0:T(1,128)S(1)}, u32[]{:S(2)}, u32[]{:S(2)}) %collective-permute-start.8) | collective-permute-done | bytes 2592 | tf_op jit(solution)/shard_map/ppermute | solution.py:378
  55.2 0.5 gather.1
  55.8 0.1 collective-permute-start.10
  55.8 1.4 %collective-permute-done.10.other_ref = f32[4,48,256]{2,1,0:T(8,128)S(1)} collective-permute-done((f32[4,48,256]{2,1,0:T(8,128)S(1)}, f32[4,48,256]{2,1,0:T(8,128)S(1)}, u32[]{:S(2)}, u32[]{:S(2)}) %collective-permute-start.10) | collective-permute-done | bytes 196640 | tf_op jit(solution)/shard_map/ppermute | solution.py:378
  57.3 1.6 %collective-permute-start.11 = (f32[48,256]{1,0:T(8,128)S(1)}, f32[48,256]{1,0:T(8,128)S(1)}, u32[]{:S(2)}, u32[]{:S(2)}) collective-permute-start(f32[48,256]{1,0:T(8,128)S(1)} %get-tuple-element.60), channel_id=1, source_target_pairs={{0,8},{4,12},{8,0},{12,4},{16,24},{20,28},{24,16},{28,20},{1,9},{5... | collective-permute-start | bytes 147464 | tf_op jit(solution)/shard_map/ppermute | solution.py:378
  58.9 1.5 %collective-permute-start.12 = (f32[48,256]{1,0:T(8,128)S(1)}, f32[48,256]{1,0:T(8,128)S(1)}, u32[]{:S(2)}, u32[]{:S(2)}) collective-permute-start(f32[48,256]{1,0:T(8,128)S(1)} %get-tuple-element.61), channel_id=1, source_target_pairs={{0,16},{4,20},{8,24},{12,28},{16,0},{20,4},{24,8},{28,12},{1,17},{... | collective-permute-start | bytes 147464 | tf_op jit(solution)/shard_map/ppermute | solution.py:378
  60.4 0.5 collective-permute-start.13
  60.9 0.6 collective-permute-done.11
  61.5 1.5 %collective-permute-done.12 = f32[48,256]{1,0:T(8,128)S(1)} collective-permute-done((f32[48,256]{1,0:T(8,128)S(1)}, f32[48,256]{1,0:T(8,128)S(1)}, u32[]{:S(2)}, u32[]{:S(2)}) %collective-permute-start.12) | collective-permute-done | bytes 49184 | tf_op jit(solution)/shard_map/ppermute | solution.py:378
  63.0 2.4 %collective-permute-done.13 = f32[48,256]{1,0:T(8,128)S(1)} collective-permute-done((f32[48,256]{1,0:T(8,128)S(1)}, f32[48,256]{1,0:T(8,128)S(1)}, u32[]{:S(2)}, u32[]{:S(2)}) %collective-permute-start.13) | collective-permute-done | bytes 49184 | tf_op jit(solution)/shard_map/ppermute | solution.py:378
  65.4 2.1 %collective-permute-start.16 = (f32[48,256]{1,0:T(8,128)S(1)}, f32[48,256]{1,0:T(8,128)S(1)}, u32[]{:S(2)}, u32[]{:S(2)}) collective-permute-start(f32[48,256]{1,0:T(8,128)S(1)} %add_add_fusion.1.refs_0_), channel_id=1, source_target_pairs={{0,3},{1,2},{2,1},{3,0},{4,7},{5,6},{6,5},{7,4},{8,11},{9,10},{10,... | collective-permute-start | bytes 147464 | tf_op jit(solution)/shard_map/ppermute | solution.py:378
  67.4 0.5 collective-permute-start.15
  67.9 1.9 %collective-permute-start.14 = (f32[48,256]{1,0:T(8,128)S(1)}, f32[48,256]{1,0:T(8,128)S(1)}, u32[]{:S(2)}, u32[]{:S(2)}) collective-permute-start(f32[48,256]{1,0:T(8,128)S(1)} %add_add_fusion.1.refs_0_), channel_id=1, source_target_pairs={{0,1},{1,0},{2,3},{3,2},{4,5},{5,4},{6,7},{7,6},{8,9},{9,8},{10,11... | collective-permute-start | bytes 147464 | tf_op jit(solution)/shard_map/ppermute | solution.py:378
  69.8 1.5 %collective-permute-done.16.refs_3_ = f32[48,256]{1,0:T(8,128)S(1)} collective-permute-done((f32[48,256]{1,0:T(8,128)S(1)}, f32[48,256]{1,0:T(8,128)S(1)}, u32[]{:S(2)}, u32[]{:S(2)}) %collective-permute-start.16) | collective-permute-done | bytes 49184 | tf_op jit(solution)/shard_map/ppermute | solution.py:378
  71.3 1.6 %collective-permute-done.15.refs_2_ = f32[48,256]{1,0:T(8,128)S(1)} collective-permute-done((f32[48,256]{1,0:T(8,128)S(1)}, f32[48,256]{1,0:T(8,128)S(1)}, u32[]{:S(2)}, u32[]{:S(2)}) %collective-permute-start.15) | collective-permute-done | bytes 49184 | tf_op jit(solution)/shard_map/ppermute | solution.py:378
  73.0 0.9 %update.1 = (f32[3,48,300]{2,1,0:T(8,128)}, f32[1,48]{1,0:T(1,128)}) custom-call(f32[3,48,300]{2,1,0:T(8,128)S(1)} %bitcast.12, f32[48,256]{1,0:T(8,128)S(1)} %add_add_fusion.1.refs_0_, f32[48,256]{1,0:T(8,128)S(1)} %collective-permute-done.14.refs_1_, f32[48,256]{1,0:T(8,128)S(1)} %collective-permute-done.15.refs_2_, ...), custom_call_target="tpu_custom_call" | custom-call | tf_op jit(solution)/shard_map/update/pallas_call | solution.py:364
  (28 shorter events, 0.1 us)
Async XLA Ops:
  0.6 3.8 %copy-start = (f32[48,3,300]{2,0,1:T(8,128)S(1)}, f32[48,3,300]{2,0,1:T(8,128)}, u32[]{:S(2)}) copy-start(f32[48,3,300]{2,0,1:T(8,128)} %param.8) | copy-start | bytes 518404
  0.6 3.7 %collective-permute-start = (f32[3,48,300]{2,1,0:T(8,128)}, f32[3,48,300]{2,1,0:T(8,128)S(1)}, u32[]{:S(2)}, u32[]{:S(2)}) collective-permute-start(f32[3,48,300]{2,1,0:T(8,128)} %bitcast.10), channel_id=1, source_target_pairs={{0,4},{4,0},{8,12},{12,8},{16,20},{20,16},{24,28},{28,24},{1,5},{5... | collective-permute-start | bytes 518408 | tf_op jit(solution)/shard_map/ppermute | solution.py:378
  1.2 1.7 %copy-start.2 = (f32[640,3,300]{0,2,1:T(8,128)S(1)}, f32[640,3,300]{0,2,1:T(8,128)}, u32[]{:S(2)}) copy-start(f32[640,3,300]{0,2,1:T(8,128)} %param.7) | copy-start | bytes 6912004
  2.8 5.8 %copy-start.1 = (bf16[11264,100]{0,1:T(8,128)(2,1)S(1)}, bf16[11264,100]{0,1:T(8,128)(2,1)}, u32[]{:S(2)}) copy-start(bf16[11264,100]{0,1:T(8,128)(2,1)} %param.13) | copy-start | bytes 6758404
  2.8 5.8 %copy-start.4 = (s32[2,11264]{1,0:T(2,128)S(1)}, s32[2,11264]{1,0:T(2,128)}, u32[]{:S(2)}) copy-start(s32[2,11264]{1,0:T(2,128)} %index_ref.1) | copy-start | bytes 270340
  2.8 5.8 %copy-start.5 = (f32[11264]{0:T(1024)S(1)}, f32[11264]{0:T(1024)}, u32[]{:S(2)}) copy-start(f32[11264]{0:T(1024)} %param.12) | copy-start | bytes 135172
  4.4 32.1 %collective-permute-start.3 = (f32[2,3,48,300]{3,2,1,0:T(8,128)S(1)}, f32[2,3,48,300]{3,2,1,0:T(8,128)S(1)}, u32[]{:S(2)}, u32[]{:S(2)}) collective-permute-start(f32[2,3,48,300]{3,2,1,0:T(8,128)S(1)} %pad_maximum_fusion.refs_0_), channel_id=1, source_target_pairs={{0,24},{4,28},{8,16},{12,20},{16,8},{20,12},{24,0},{28,4},{1,25},{... | collective-permute-start | bytes 1036808 | tf_op jit(solution)/shard_map/ppermute | solution.py:378
  8.0 28.5 %collective-permute-start.2 = (f32[2,3,48,300]{3,2,1,0:T(8,128)S(1)}, f32[2,3,48,300]{3,2,1,0:T(8,128)S(1)}, u32[]{:S(2)}, u32[]{:S(2)}) collective-permute-start(f32[2,3,48,300]{3,2,1,0:T(8,128)S(1)} %pad_maximum_fusion.refs_0_), channel_id=1, source_target_pairs={{0,16},{4,20},{8,24},{12,28},{16,0},{20,4},{24,8},{28,12},{1,17},{... | collective-permute-start | bytes 1036808 | tf_op jit(solution)/shard_map/ppermute | solution.py:378
  8.5 28.1 %collective-permute-start.1 = (f32[2,3,48,300]{3,2,1,0:T(8,128)S(1)}, f32[2,3,48,300]{3,2,1,0:T(8,128)S(1)}, u32[]{:S(2)}, u32[]{:S(2)}) collective-permute-start(f32[2,3,48,300]{3,2,1,0:T(8,128)S(1)} %pad_maximum_fusion.refs_0_), channel_id=1, source_target_pairs={{0,8},{4,12},{8,0},{12,4},{16,24},{20,28},{24,16},{28,20},{1,9},{5... | collective-permute-start | bytes 1036808 | tf_op jit(solution)/shard_map/ppermute | solution.py:378
  8.6 32.6 %copy-start.3 = (f32[640,3,300]{0,2,1:T(8,128)S(1)}, f32[640,3,300]{0,2,1:T(8,128)}, u32[]{:S(2)}) copy-start(f32[640,3,300]{0,2,1:T(8,128)} %param.7) | copy-start | bytes 6912004
  8.7 32.5 %copy-start.6 = (s32[640]{0:T(1024)S(1)}, s32[640]{0:T(1024)}, u32[]{:S(2)}) copy-start(s32[640]{0:T(1024)} %assigned_ref.1) | copy-start | bytes 7684
  8.7 32.5 %copy-start.7 = (s32[384]{0:T(512)S(1)}, s32[384]{0:T(512)}, u32[]{:S(2)}) copy-start(s32[384]{0:T(512)} %home_ref.1) | copy-start | bytes 4612
  36.6 7.8 %collective-permute-start.4 = (f32[25,640]{1,0:T(8,128)S(1)}, f32[25,640]{1,0:T(8,128)S(1)}, u32[]{:S(2)}, u32[]{:S(2)}) collective-permute-start(f32[25,640]{1,0:T(8,128)S(1)} %get-tuple-element.49), channel_id=1, source_target_pairs={{0,1},{1,0},{2,3},{3,2},{4,5},{5,4},{6,7},{7,6},{8,9},{9,8},{10,11... | collective-permute-start | bytes 192008 | tf_op jit(solution)/shard_map/ppermute | solution.py:378
  38.6 9.0 %collective-permute-start.5 = (f32[25,640]{1,0:T(8,128)S(1)}, f32[25,640]{1,0:T(8,128)S(1)}, u32[]{:S(2)}, u32[]{:S(2)}) collective-permute-start(f32[25,640]{1,0:T(8,128)S(1)} %get-tuple-element.50), channel_id=1, source_target_pairs={{0,2},{1,3},{2,0},{3,1},{4,6},{5,7},{6,4},{7,5},{8,10},{9,11},{10,... | collective-permute-start | bytes 192008 | tf_op jit(solution)/shard_map/ppermute | solution.py:378
  41.2 6.4 %collective-permute-start.6 = (f32[25,640]{1,0:T(8,128)S(1)}, f32[25,640]{1,0:T(8,128)S(1)}, u32[]{:S(2)}, u32[]{:S(2)}) collective-permute-start(f32[25,640]{1,0:T(8,128)S(1)} %get-tuple-element.51), channel_id=1, source_target_pairs={{0,3},{1,2},{2,1},{3,0},{4,7},{5,6},{6,5},{7,4},{8,11},{9,10},{10,... | collective-permute-start | bytes 192008 | tf_op jit(solution)/shard_map/ppermute | solution.py:378
  48.3 5.4 %collective-permute-start.9 = (f32[1,640]{1,0:T(1,128)S(1)}, f32[1,640]{1,0:T(1,128)S(1)}, u32[]{:S(2)}, u32[]{:S(2)}) collective-permute-start(f32[1,640]{1,0:T(1,128)S(1)} %broadcast_in_dim.7.refs_0_), channel_id=1, source_target_pairs={{0,3},{1,2},{2,1},{3,0},{4,7},{5,6},{6,5},{7,4},{8,11},{9,10},{10,... | collective-permute-start | bytes 7688 | tf_op jit(solution)/shard_map/ppermute | solution.py:378
  50.7 4.5 %collective-permute-start.8 = (f32[1,640]{1,0:T(1,128)S(1)}, f32[1,640]{1,0:T(1,128)S(1)}, u32[]{:S(2)}, u32[]{:S(2)}) collective-permute-start(f32[1,640]{1,0:T(1,128)S(1)} %broadcast_in_dim.7.refs_0_), channel_id=1, source_target_pairs={{0,2},{1,3},{2,0},{3,1},{4,6},{5,7},{6,4},{7,5},{8,10},{9,11},{10,... | collective-permute-start | bytes 7688 | tf_op jit(solution)/shard_map/ppermute | solution.py:378
  51.2 4.1 %collective-permute-start.7 = (f32[1,640]{1,0:T(1,128)S(1)}, f32[1,640]{1,0:T(1,128)S(1)}, u32[]{:S(2)}, u32[]{:S(2)}) collective-permute-start(f32[1,640]{1,0:T(1,128)S(1)} %broadcast_in_dim.7.refs_0_), channel_id=1, source_target_pairs={{0,1},{1,0},{2,3},{3,2},{4,5},{5,4},{6,7},{7,6},{8,9},{9,8},{10,11... | collective-permute-start | bytes 7688 | tf_op jit(solution)/shard_map/ppermute | solution.py:378
  55.8 1.5 %collective-permute-start.10 = (f32[4,48,256]{2,1,0:T(8,128)S(1)}, f32[4,48,256]{2,1,0:T(8,128)S(1)}, u32[]{:S(2)}, u32[]{:S(2)}) collective-permute-start(f32[4,48,256]{2,1,0:T(8,128)S(1)} %get-tuple-element.58), channel_id=1, source_target_pairs={{0,4},{4,0},{8,12},{12,8},{16,20},{20,16},{24,28},{28,24},{1,5},{5... | collective-permute-start | bytes 589832 | tf_op jit(solution)/shard_map/ppermute | solution.py:378
  57.3 4.2 %collective-permute-start.11 = (f32[48,256]{1,0:T(8,128)S(1)}, f32[48,256]{1,0:T(8,128)S(1)}, u32[]{:S(2)}, u32[]{:S(2)}) collective-permute-start(f32[48,256]{1,0:T(8,128)S(1)} %get-tuple-element.60), channel_id=1, source_target_pairs={{0,8},{4,12},{8,0},{12,4},{16,24},{20,28},{24,16},{28,20},{1,9},{5... | collective-permute-start | bytes 147464 | tf_op jit(solution)/shard_map/ppermute | solution.py:378
  58.9 4.1 %collective-permute-start.12 = (f32[48,256]{1,0:T(8,128)S(1)}, f32[48,256]{1,0:T(8,128)S(1)}, u32[]{:S(2)}, u32[]{:S(2)}) collective-permute-start(f32[48,256]{1,0:T(8,128)S(1)} %get-tuple-element.61), channel_id=1, source_target_pairs={{0,16},{4,20},{8,24},{12,28},{16,0},{20,4},{24,8},{28,12},{1,17},{... | collective-permute-start | bytes 147464 | tf_op jit(solution)/shard_map/ppermute | solution.py:378
  60.4 5.0 %collective-permute-start.13 = (f32[48,256]{1,0:T(8,128)S(1)}, f32[48,256]{1,0:T(8,128)S(1)}, u32[]{:S(2)}, u32[]{:S(2)}) collective-permute-start(f32[48,256]{1,0:T(8,128)S(1)} %get-tuple-element.62), channel_id=1, source_target_pairs={{0,24},{4,28},{8,16},{12,20},{16,8},{20,12},{24,0},{28,4},{1,25},{... | collective-permute-start | bytes 147464 | tf_op jit(solution)/shard_map/ppermute | solution.py:378
  65.4 6.0 %collective-permute-start.16 = (f32[48,256]{1,0:T(8,128)S(1)}, f32[48,256]{1,0:T(8,128)S(1)}, u32[]{:S(2)}, u32[]{:S(2)}) collective-permute-start(f32[48,256]{1,0:T(8,128)S(1)} %add_add_fusion.1.refs_0_), channel_id=1, source_target_pairs={{0,3},{1,2},{2,1},{3,0},{4,7},{5,6},{6,5},{7,4},{8,11},{9,10},{10,... | collective-permute-start | bytes 147464 | tf_op jit(solution)/shard_map/ppermute | solution.py:378
  67.4 5.5 %collective-permute-start.15 = (f32[48,256]{1,0:T(8,128)S(1)}, f32[48,256]{1,0:T(8,128)S(1)}, u32[]{:S(2)}, u32[]{:S(2)}) collective-permute-start(f32[48,256]{1,0:T(8,128)S(1)} %add_add_fusion.1.refs_0_), channel_id=1, source_target_pairs={{0,2},{1,3},{2,0},{3,1},{4,6},{5,7},{6,4},{7,5},{8,10},{9,11},{10,... | collective-permute-start | bytes 147464 | tf_op jit(solution)/shard_map/ppermute | solution.py:378
  67.9 5.0 %collective-permute-start.14 = (f32[48,256]{1,0:T(8,128)S(1)}, f32[48,256]{1,0:T(8,128)S(1)}, u32[]{:S(2)}, u32[]{:S(2)}) collective-permute-start(f32[48,256]{1,0:T(8,128)S(1)} %add_add_fusion.1.refs_0_), channel_id=1, source_target_pairs={{0,1},{1,0},{2,3},{3,2},{4,5},{5,4},{6,7},{7,6},{8,9},{9,8},{10,11... | collective-permute-start | bytes 147464 | tf_op jit(solution)/shard_map/ppermute | solution.py:378

commit v3 on v2

--- a/solution.py
+++ b/solution.py
@@ -143,7 +143,8 @@
             value = rows[0]
             for k in range(1, parts):
                 value = jnp.where(me ^ s == k, rows[k], value)
-            out_ref[...] = value
+            for j in range(frames // LANES):
+                out_ref[j * share : (j + 1) * share, :] = value[:, j * LANES : (j + 1) * LANES]
 
 
 def project(positions, unit, res_count, pair_index, mean_dist, tica_weight, axis):
@@ -163,8 +164,8 @@
             pl.BlockSpec(positions.shape, lambda i: (0, 0)),
             pl.BlockSpec(unit.shape, lambda i: (0, 0)),
         ],
-        out_specs=[pl.BlockSpec((share, frames), lambda i: (0, 0))] * parts,
-        out_shape=[jax.ShapeDtypeStruct((share, frames), jnp.float32)] * parts,
+        out_specs=[pl.BlockSpec((share * frames // LANES, LANES), lambda i: (0, 0))] * parts,
+        out_shape=[jax.ShapeDtypeStruct((share * frames // LANES, LANES), jnp.float32)] * parts,
         scratch_shapes=[
             pltpu.VMEM((depth, block), piece_type),
             pltpu.VMEM((frames, round_up(comps, 128)), jnp.float32),
@@ -177,6 +178,29 @@
         ),
         name="project",
     )(pair_index, mean_dist, tica_weight, positions, unit)
+
+
+def finish_kernel(*refs):
+    part_refs, (tica_ref, square_ref) = refs[:-2], refs[-2:]
+    share, frames = tica_ref.shape
+    total = sum(ref[...] for ref in part_refs)
+    for j in range(frames // LANES):
+        part = total[j * share : (j + 1) * share, :]
+        tica_ref[:, j * LANES : (j + 1) * LANES] = part
+        square_ref[:, j * LANES : (j + 1) * LANES] = jnp.sum(part * part, axis=0, keepdims=True)
+
+
+def finish(partial, frames):
+    share = partial[0].size // frames
+    return pl.pallas_call(
+        finish_kernel,
+        out_shape=[
+            jax.ShapeDtypeStruct((share, frames), jnp.float32),
+            jax.ShapeDtypeStruct((1, frames), jnp.float32),
+        ],
+        compiler_params=pltpu.CompilerParams(vmem_limit_bytes=8 * MIB),
+        name="finish",
+    )(*partial)
 
 
 def polar_factor(cross):
@@ -398,17 +422,15 @@
         positions, unit, coords.shape[1], pair_index, mean_dist[None, :], tica_weight.T, "pairs"
     )
     partial, refs = lax.optimization_barrier((partial, refs))
-    received = [swap(partial[s], "pairs", s) for s in range(1, parts)]
+    received = [swap(partial[s], "pairs", s) for s in reversed(range(1, parts))]
     member, aligned, received = lax.optimization_barrier(
         (
             *align(coords, assignment, home_row, refs, "frames", "pairs", quarter),
             received,
         )
     )
-    tica = partial[0]
-    for piece in received:
-        tica = tica + piece
-    squares = gathered(jnp.sum(tica * tica, axis=0, keepdims=True), "pairs")
+    tica, square = finish([partial[0], *received], coords.shape[2])
+    squares = gathered(square, "pairs")
     mine, other = gather(member, aligned, squares, "pairs", "frames", comps)
     sums = merge(mine, swap(other, "frames", 1))
     total = sums[0]

time: 74.1 us -> 72.2 us (0.974)
  waiting for transfers between devices: 14.9 us -> 13 us
    ppermute x17, waiting for transfers between devices: 14.9 us -> 13 us  [swap(): return lax.ppermute(value, axis, [(i, i ^ step) for i in range(size)])]
  transfers between devices with their start and end apart: 17 -> 17, of which waited for: 9 -> 10; matrix products, arithmetic and copies ran while one was open for 0% -> 0% of each run, Pallas kernels for 44% -> 45%
where the time goes in v3:
time: 72.2 us; the launch traced here: 72 us
  Pallas kernels  34.6 us (48%)
  starting transfers between devices  21.9 us (30%)
  waiting for transfers between devices  13 us (18%)
  local copies, waits for them, and re-layouts  1.69 us (2%)
  between operations  0.78 us (1%)
    pallas_call x1, Pallas kernels, project(): pl.pallas_call(functools.partial(project_kernel, axis, share, res_count),...  27.8 us
    ppermute x17, starting transfers between devices, swap(): return lax.ppermute(value, axis, [(i, i ^ step) for i in range(size)])  21.9 us
    ppermute x17, waiting for transfers between devices, swap(): return lax.ppermute(value, axis, [(i, i ^ step) for i in range(size)])  13 us
    pallas_call x1, Pallas kernels, align(): pl.pallas_call(functools.partial(align_kernel, frames_axis, pairs_axis, q...  3.09 us
    unnamed x16, local copies, waits for them, and re-layouts  1.69 us
    pallas_call x1, Pallas kernels, split_coords(): pl.pallas_call(split_kernel, out_shape=[jax.ShapeDtypeStruct((dims * fram...  1.55 us
  transfers between devices with their start and end apart: 17, of which 10 were waited for; matrix products, arithmetic and copies ran while one was open for 0% of the time, Pallas kernels for 45%

profile of v3, /device:TPU:0, one launch (start us, length us, event | category | flops | bytes accessed | tf_op | source)
XLA Modules:
  0.0 72.0 jit_solution(13806628378834616744)
XLA Ops:
  0.6 0.5 collective-permute-start
  1.2 1.7 %copy-done.2 = f32[640,3,300]{0,2,1:T(8,128)S(1)} copy-done((f32[640,3,300]{0,2,1:T(8,128)S(1)}, f32[640,3,300]{0,2,1:T(8,128)}, u32[]{:S(2)}) %copy-start.2) | copy-done | bytes 2304024
  2.8 1.6 %split.1 = (f8e4m3fn[1920,1024]{1,0:T(32,128)(4,1)S(1)}, f32[640,128]{1,0:T(8,128)S(1)}) custom-call(f32[3,300,640]{2,1,0:T(8,128)S(1)} %bitcast.14), custom_call_target="tpu_custom_call" | custom-call | flops 1073741824 | bytes 8388608 | tf_op jit(solution)/shard_map/split/pallas_call | solution.py:73
  4.4 3.6 %collective-permute-start.3 = (f32[2,3,48,300]{3,2,1,0:T(8,128)S(1)}, f32[2,3,48,300]{3,2,1,0:T(8,128)S(1)}, u32[]{:S(2)}, u32[]{:S(2)}) collective-permute-start(f32[2,3,48,300]{3,2,1,0:T(8,128)S(1)} %pad_maximum_fusion.refs_0_), channel_id=1, source_target_pairs={{0,24},{4,28},{8,16},{12,20},{16,8},{20,12},{24,0},{28,4},{1,25},{... | collective-permute-start | bytes 1036808 | tf_op jit(solution)/shard_map/ppermute | solution.py:402
  8.0 0.5 collective-permute-start.2
  8.5 0.1 collective-permute-start.1
  8.7 27.8 %project.1 = (f32[125,128]{1,0:T(8,128)S(1)}, f32[125,128]{1,0:T(8,128)S(1)}, f32[125,128]{1,0:T(8,128)S(1)}, f32[125,128]{1,0:T(8,128)S(1)}) custom-call(s32[2,11264]{1,0:T(2,128)S(1)} %copy-done.4, f32[1,11264]{1,0:T(1,128)S(1)} %bitcast.16, bf16[100,11264]{1,0:T(8,128)(2,1)S(1)} %bitcast.13, f8e4m3fn[1920,1024]{1,0:T(32,128)(4,1)S(1)} %get-tuple-element.37.positions_ref, ...), custom_call_target="tpu_custom_call" | custom-call | flops 44291850240 | bytes 8388608 | tf_op jit(solution)/shard_map/project/pallas_call | solution.py:157
  36.6 4.1 %collective-permute-start.4 = (f32[125,128]{1,0:T(8,128)S(1)}, f32[125,128]{1,0:T(8,128)S(1)}, u32[]{:S(2)}, u32[]{:S(2)}) collective-permute-start(f32[125,128]{1,0:T(8,128)S(1)} %get-tuple-element.51), channel_id=1, source_target_pairs={{0,3},{1,2},{2,1},{3,0},{4,7},{5,6},{6,5},{7,4},{8,11},{9,10},{10,... | collective-permute-start | bytes 192008 | tf_op jit(solution)/shard_map/ppermute | solution.py:402
  40.6 0.6 collective-permute-start.6
  41.3 3.1 %align.1 = (bf16[384,640]{1,0:T(8,128)(2,1)S(1)}, f32[240,640]{1,0:T(8,128)S(1)}) custom-call(f32[3,300,640]{2,1,0:T(8,128)S(1)} %bitcast.15, s32[640]{0:T(1024)S(1)} %copy-done.6, s32[384]{0:T(512)S(1)} %copy-done.7, f32[2,3,48,300]{3,2,1,0:T(8,128)S(1)} %pad_maximum_fusion.refs_0_, f32[2,3,48,300]{3,2,1,0:T(8,128)S(1)} %collective-permute-done.1.refs_1_, ...), custom_call_target="tpu_custom_call" | custom-call | flops 1769472000 | bytes 4194304 | tf_op jit(solution)/shard_map/align/pallas_call | solution.py:284
  44.4 1.6 %collective-permute-done.5.refs_2_ = f32[125,128]{1,0:T(8,128)S(1)} collective-permute-done((f32[125,128]{1,0:T(8,128)S(1)}, f32[125,128]{1,0:T(8,128)S(1)}, u32[]{:S(2)}, u32[]{:S(2)}) %collective-permute-start.5) | collective-permute-done | bytes 64032 | tf_op jit(solution)/shard_map/ppermute | solution.py:402
  46.0 0.7 finish.1
  46.7 2.7 %collective-permute-start.9 = (f32[1,640]{1,0:T(1,128)S(1)}, f32[1,640]{1,0:T(1,128)S(1)}, u32[]{:S(2)}, u32[]{:S(2)}) collective-permute-start(f32[1,640]{1,0:T(1,128)S(1)} %get-tuple-element.60.refs_0_), channel_id=1, source_target_pairs={{0,3},{1,2},{2,1},{3,0},{4,7},{5,6},{6,5},{7,4},{8,11},{9,10},{10,... | collective-permute-start | bytes 7688 | tf_op jit(solution)/shard_map/ppermute | solution.py:402
  49.4 1.7 %collective-permute-start.7 = (f32[1,640]{1,0:T(1,128)S(1)}, f32[1,640]{1,0:T(1,128)S(1)}, u32[]{:S(2)}, u32[]{:S(2)}) collective-permute-start(f32[1,640]{1,0:T(1,128)S(1)} %get-tuple-element.60.refs_0_), channel_id=1, source_target_pairs={{0,1},{1,0},{2,3},{3,2},{4,5},{5,4},{6,7},{7,6},{8,9},{9,8},{10,11... | collective-permute-start | bytes 7688 | tf_op jit(solution)/shard_map/ppermute | solution.py:402
  51.1 1.0 %collective-permute-done.9.refs_3_ = f32[1,640]{1,0:T(1,128)S(1)} collective-permute-done((f32[1,640]{1,0:T(1,128)S(1)}, f32[1,640]{1,0:T(1,128)S(1)}, u32[]{:S(2)}, u32[]{:S(2)}) %collective-permute-start.9) | collective-permute-done | bytes 2592 | tf_op jit(solution)/shard_map/ppermute | solution.py:402
  52.1 1.8 %collective-permute-done.8.refs_2_ = f32[1,640]{1,0:T(1,128)S(1)} collective-permute-done((f32[1,640]{1,0:T(1,128)S(1)}, f32[1,640]{1,0:T(1,128)S(1)}, u32[]{:S(2)}, u32[]{:S(2)}) %collective-permute-start.8) | collective-permute-done | bytes 2592 | tf_op jit(solution)/shard_map/ppermute | solution.py:402
  53.9 0.5 gather.1
  54.4 0.1 collective-permute-start.10
  54.5 1.4 %collective-permute-done.10.other_ref = f32[4,48,256]{2,1,0:T(8,128)S(1)} collective-permute-done((f32[4,48,256]{2,1,0:T(8,128)S(1)}, f32[4,48,256]{2,1,0:T(8,128)S(1)}, u32[]{:S(2)}, u32[]{:S(2)}) %collective-permute-start.10) | collective-permute-done | bytes 196640 | tf_op jit(solution)/shard_map/ppermute | solution.py:402
  56.0 1.6 %collective-permute-start.11 = (f32[48,256]{1,0:T(8,128)S(1)}, f32[48,256]{1,0:T(8,128)S(1)}, u32[]{:S(2)}, u32[]{:S(2)}) collective-permute-start(f32[48,256]{1,0:T(8,128)S(1)} %get-tuple-element.64), channel_id=1, source_target_pairs={{0,8},{4,12},{8,0},{12,4},{16,24},{20,28},{24,16},{28,20},{1,9},{5... | collective-permute-start | bytes 147464 | tf_op jit(solution)/shard_map/ppermute | solution.py:402
  57.5 1.5 %collective-permute-start.12 = (f32[48,256]{1,0:T(8,128)S(1)}, f32[48,256]{1,0:T(8,128)S(1)}, u32[]{:S(2)}, u32[]{:S(2)}) collective-permute-start(f32[48,256]{1,0:T(8,128)S(1)} %get-tuple-element.65), channel_id=1, source_target_pairs={{0,16},{4,20},{8,24},{12,28},{16,0},{20,4},{24,8},{28,12},{1,17},{... | collective-permute-start | bytes 147464 | tf_op jit(solution)/shard_map/ppermute | solution.py:402
  59.0 0.5 collective-permute-start.13
  59.5 0.6 collective-permute-done.11
  60.1 1.5 %collective-permute-done.12 = f32[48,256]{1,0:T(8,128)S(1)} collective-permute-done((f32[48,256]{1,0:T(8,128)S(1)}, f32[48,256]{1,0:T(8,128)S(1)}, u32[]{:S(2)}, u32[]{:S(2)}) %collective-permute-start.12) | collective-permute-done | bytes 49184 | tf_op jit(solution)/shard_map/ppermute | solution.py:402
  61.6 2.4 %collective-permute-done.13 = f32[48,256]{1,0:T(8,128)S(1)} collective-permute-done((f32[48,256]{1,0:T(8,128)S(1)}, f32[48,256]{1,0:T(8,128)S(1)}, u32[]{:S(2)}, u32[]{:S(2)}) %collective-permute-start.13) | collective-permute-done | bytes 49184 | tf_op jit(solution)/shard_map/ppermute | solution.py:402
  64.1 1.5 %collective-permute-start.16 = (f32[48,256]{1,0:T(8,128)S(1)}, f32[48,256]{1,0:T(8,128)S(1)}, u32[]{:S(2)}, u32[]{:S(2)}) collective-permute-start(f32[48,256]{1,0:T(8,128)S(1)} %add_add_fusion.refs_0_), channel_id=1, source_target_pairs={{0,3},{1,2},{2,1},{3,0},{4,7},{5,6},{6,5},{7,4},{8,11},{9,10},{10,... | collective-permute-start | bytes 147464 | tf_op jit(solution)/shard_map/ppermute | solution.py:402
  65.6 0.9 %collective-permute-start.15 = (f32[48,256]{1,0:T(8,128)S(1)}, f32[48,256]{1,0:T(8,128)S(1)}, u32[]{:S(2)}, u32[]{:S(2)}) collective-permute-start(f32[48,256]{1,0:T(8,128)S(1)} %add_add_fusion.refs_0_), channel_id=1, source_target_pairs={{0,2},{1,3},{2,0},{3,1},{4,6},{5,7},{6,4},{7,5},{8,10},{9,11},{10,... | collective-permute-start | bytes 147464 | tf_op jit(solution)/shard_map/ppermute | solution.py:402
  66.5 2.1 %collective-permute-start.14 = (f32[48,256]{1,0:T(8,128)S(1)}, f32[48,256]{1,0:T(8,128)S(1)}, u32[]{:S(2)}, u32[]{:S(2)}) collective-permute-start(f32[48,256]{1,0:T(8,128)S(1)} %add_add_fusion.refs_0_), channel_id=1, source_target_pairs={{0,1},{1,0},{2,3},{3,2},{4,5},{5,4},{6,7},{7,6},{8,9},{9,8},{10,11... | collective-permute-start | bytes 147464 | tf_op jit(solution)/shard_map/ppermute | solution.py:402
  68.5 1.5 %collective-permute-done.16.refs_3_ = f32[48,256]{1,0:T(8,128)S(1)} collective-permute-done((f32[48,256]{1,0:T(8,128)S(1)}, f32[48,256]{1,0:T(8,128)S(1)}, u32[]{:S(2)}, u32[]{:S(2)}) %collective-permute-start.16) | collective-permute-done | bytes 49184 | tf_op jit(solution)/shard_map/ppermute | solution.py:402
  70.0 0.6 collective-permute-done.15.refs_2_
  70.6 0.5 collective-permute-done.14.refs_1_
  71.1 0.9 %update.1 = (f32[3,48,300]{2,1,0:T(8,128)}, f32[1,48]{1,0:T(1,128)}) custom-call(f32[3,48,300]{2,1,0:T(8,128)S(1)} %bitcast.12, f32[48,256]{1,0:T(8,128)S(1)} %add_add_fusion.refs_0_, f32[48,256]{1,0:T(8,128)S(1)} %collective-permute-done.14.refs_1_, f32[48,256]{1,0:T(8,128)S(1)} %collective-permute-done.15.refs_2_, ...), custom_call_target="tpu_custom_call" | custom-call | tf_op jit(solution)/shard_map/update/pallas_call | solution.py:388
  (27 shorter events, 0.1 us)
Async XLA Ops:
  0.6 3.8 %copy-start = (f32[48,3,300]{2,0,1:T(8,128)S(1)}, f32[48,3,300]{2,0,1:T(8,128)}, u32[]{:S(2)}) copy-start(f32[48,3,300]{2,0,1:T(8,128)} %param.8) | copy-start | bytes 518404
  0.6 3.7 %collective-permute-start = (f32[3,48,300]{2,1,0:T(8,128)}, f32[3,48,300]{2,1,0:T(8,128)S(1)}, u32[]{:S(2)}, u32[]{:S(2)}) collective-permute-start(f32[3,48,300]{2,1,0:T(8,128)} %bitcast.10), channel_id=1, source_target_pairs={{0,4},{4,0},{8,12},{12,8},{16,20},{20,16},{24,28},{28,24},{1,5},{5... | collective-permute-start | bytes 518408 | tf_op jit(solution)/shard_map/ppermute | solution.py:402
  1.2 1.7 %copy-start.2 = (f32[640,3,300]{0,2,1:T(8,128)S(1)}, f32[640,3,300]{0,2,1:T(8,128)}, u32[]{:S(2)}) copy-start(f32[640,3,300]{0,2,1:T(8,128)} %param.7) | copy-start | bytes 6912004
  2.8 5.8 %copy-start.1 = (bf16[11264,100]{0,1:T(8,128)(2,1)S(1)}, bf16[11264,100]{0,1:T(8,128)(2,1)}, u32[]{:S(2)}) copy-start(bf16[11264,100]{0,1:T(8,128)(2,1)} %param.13) | copy-start | bytes 6758404
  2.8 5.8 %copy-start.4 = (s32[2,11264]{1,0:T(2,128)S(1)}, s32[2,11264]{1,0:T(2,128)}, u32[]{:S(2)}) copy-start(s32[2,11264]{1,0:T(2,128)} %index_ref.1) | copy-start | bytes 270340
  2.8 5.8 %copy-start.5 = (f32[11264]{0:T(1024)S(1)}, f32[11264]{0:T(1024)}, u32[]{:S(2)}) copy-start(f32[11264]{0:T(1024)} %param.12) | copy-start | bytes 135172
  4.4 32.1 %collective-permute-start.3 = (f32[2,3,48,300]{3,2,1,0:T(8,128)S(1)}, f32[2,3,48,300]{3,2,1,0:T(8,128)S(1)}, u32[]{:S(2)}, u32[]{:S(2)}) collective-permute-start(f32[2,3,48,300]{3,2,1,0:T(8,128)S(1)} %pad_maximum_fusion.refs_0_), channel_id=1, source_target_pairs={{0,24},{4,28},{8,16},{12,20},{16,8},{20,12},{24,0},{28,4},{1,25},{... | collective-permute-start | bytes 1036808 | tf_op jit(solution)/shard_map/ppermute | solution.py:402
  8.0 28.5 %collective-permute-start.2 = (f32[2,3,48,300]{3,2,1,0:T(8,128)S(1)}, f32[2,3,48,300]{3,2,1,0:T(8,128)S(1)}, u32[]{:S(2)}, u32[]{:S(2)}) collective-permute-start(f32[2,3,48,300]{3,2,1,0:T(8,128)S(1)} %pad_maximum_fusion.refs_0_), channel_id=1, source_target_pairs={{0,16},{4,20},{8,24},{12,28},{16,0},{20,4},{24,8},{28,12},{1,17},{... | collective-permute-start | bytes 1036808 | tf_op jit(solution)/shard_map/ppermute | solution.py:402
  8.5 28.0 %collective-permute-start.1 = (f32[2,3,48,300]{3,2,1,0:T(8,128)S(1)}, f32[2,3,48,300]{3,2,1,0:T(8,128)S(1)}, u32[]{:S(2)}, u32[]{:S(2)}) collective-permute-start(f32[2,3,48,300]{3,2,1,0:T(8,128)S(1)} %pad_maximum_fusion.refs_0_), channel_id=1, source_target_pairs={{0,8},{4,12},{8,0},{12,4},{16,24},{20,28},{24,16},{28,20},{1,9},{5... | collective-permute-start | bytes 1036808 | tf_op jit(solution)/shard_map/ppermute | solution.py:402
  8.6 32.6 %copy-start.3 = (f32[640,3,300]{0,2,1:T(8,128)S(1)}, f32[640,3,300]{0,2,1:T(8,128)}, u32[]{:S(2)}) copy-start(f32[640,3,300]{0,2,1:T(8,128)} %param.7) | copy-start | bytes 6912004
  8.7 32.6 %copy-start.6 = (s32[640]{0:T(1024)S(1)}, s32[640]{0:T(1024)}, u32[]{:S(2)}) copy-start(s32[640]{0:T(1024)} %assigned_ref.1) | copy-start | bytes 7684
  8.7 32.6 %copy-start.7 = (s32[384]{0:T(512)S(1)}, s32[384]{0:T(512)}, u32[]{:S(2)}) copy-start(s32[384]{0:T(512)} %home_ref.1) | copy-start | bytes 4612
  36.6 7.8 %collective-permute-start.4 = (f32[125,128]{1,0:T(8,128)S(1)}, f32[125,128]{1,0:T(8,128)S(1)}, u32[]{:S(2)}, u32[]{:S(2)}) collective-permute-start(f32[125,128]{1,0:T(8,128)S(1)} %get-tuple-element.51), channel_id=1, source_target_pairs={{0,3},{1,2},{2,1},{3,0},{4,7},{5,6},{6,5},{7,4},{8,11},{9,10},{10,... | collective-permute-start | bytes 192008 | tf_op jit(solution)/shard_map/ppermute | solution.py:402
  40.6 5.4 %collective-permute-start.5 = (f32[125,128]{1,0:T(8,128)S(1)}, f32[125,128]{1,0:T(8,128)S(1)}, u32[]{:S(2)}, u32[]{:S(2)}) collective-permute-start(f32[125,128]{1,0:T(8,128)S(1)} %get-tuple-element.52), channel_id=1, source_target_pairs={{0,2},{1,3},{2,0},{3,1},{4,6},{5,7},{6,4},{7,5},{8,10},{9,11},{10,... | collective-permute-start | bytes 192008 | tf_op jit(solution)/shard_map/ppermute | solution.py:402
  40.6 5.4 %collective-permute-start.6 = (f32[125,128]{1,0:T(8,128)S(1)}, f32[125,128]{1,0:T(8,128)S(1)}, u32[]{:S(2)}, u32[]{:S(2)}) collective-permute-start(f32[125,128]{1,0:T(8,128)S(1)} %get-tuple-element.53), channel_id=1, source_target_pairs={{0,1},{1,0},{2,3},{3,2},{4,5},{5,4},{6,7},{7,6},{8,9},{9,8},{10,11... | collective-permute-start | bytes 192008 | tf_op jit(solution)/shard_map/ppermute | solution.py:402
  46.7 5.4 %collective-permute-start.9 = (f32[1,640]{1,0:T(1,128)S(1)}, f32[1,640]{1,0:T(1,128)S(1)}, u32[]{:S(2)}, u32[]{:S(2)}) collective-permute-start(f32[1,640]{1,0:T(1,128)S(1)} %get-tuple-element.60.refs_0_), channel_id=1, source_target_pairs={{0,3},{1,2},{2,1},{3,0},{4,7},{5,6},{6,5},{7,4},{8,11},{9,10},{10,... | collective-permute-start | bytes 7688 | tf_op jit(solution)/shard_map/ppermute | solution.py:402
  49.4 4.5 %collective-permute-start.8 = (f32[1,640]{1,0:T(1,128)S(1)}, f32[1,640]{1,0:T(1,128)S(1)}, u32[]{:S(2)}, u32[]{:S(2)}) collective-permute-start(f32[1,640]{1,0:T(1,128)S(1)} %get-tuple-element.60.refs_0_), channel_id=1, source_target_pairs={{0,2},{1,3},{2,0},{3,1},{4,6},{5,7},{6,4},{7,5},{8,10},{9,11},{10,... | collective-permute-start | bytes 7688 | tf_op jit(solution)/shard_map/ppermute | solution.py:402
  49.4 4.5 %collective-permute-start.7 = (f32[1,640]{1,0:T(1,128)S(1)}, f32[1,640]{1,0:T(1,128)S(1)}, u32[]{:S(2)}, u32[]{:S(2)}) collective-permute-start(f32[1,640]{1,0:T(1,128)S(1)} %get-tuple-element.60.refs_0_), channel_id=1, source_target_pairs={{0,1},{1,0},{2,3},{3,2},{4,5},{5,4},{6,7},{7,6},{8,9},{9,8},{10,11... | collective-permute-start | bytes 7688 | tf_op jit(solution)/shard_map/ppermute | solution.py:402
  54.4 1.5 %collective-permute-start.10 = (f32[4,48,256]{2,1,0:T(8,128)S(1)}, f32[4,48,256]{2,1,0:T(8,128)S(1)}, u32[]{:S(2)}, u32[]{:S(2)}) collective-permute-start(f32[4,48,256]{2,1,0:T(8,128)S(1)} %get-tuple-element.62), channel_id=1, source_target_pairs={{0,4},{4,0},{8,12},{12,8},{16,20},{20,16},{24,28},{28,24},{1,5},{5... | collective-permute-start | bytes 589832 | tf_op jit(solution)/shard_map/ppermute | solution.py:402
  56.0 4.2 %collective-permute-start.11 = (f32[48,256]{1,0:T(8,128)S(1)}, f32[48,256]{1,0:T(8,128)S(1)}, u32[]{:S(2)}, u32[]{:S(2)}) collective-permute-start(f32[48,256]{1,0:T(8,128)S(1)} %get-tuple-element.64), channel_id=1, source_target_pairs={{0,8},{4,12},{8,0},{12,4},{16,24},{20,28},{24,16},{28,20},{1,9},{5... | collective-permute-start | bytes 147464 | tf_op jit(solution)/shard_map/ppermute | solution.py:402
  57.5 4.1 %collective-permute-start.12 = (f32[48,256]{1,0:T(8,128)S(1)}, f32[48,256]{1,0:T(8,128)S(1)}, u32[]{:S(2)}, u32[]{:S(2)}) collective-permute-start(f32[48,256]{1,0:T(8,128)S(1)} %get-tuple-element.65), channel_id=1, source_target_pairs={{0,16},{4,20},{8,24},{12,28},{16,0},{20,4},{24,8},{28,12},{1,17},{... | collective-permute-start | bytes 147464 | tf_op jit(solution)/shard_map/ppermute | solution.py:402
  59.0 5.0 %collective-permute-start.13 = (f32[48,256]{1,0:T(8,128)S(1)}, f32[48,256]{1,0:T(8,128)S(1)}, u32[]{:S(2)}, u32[]{:S(2)}) collective-permute-start(f32[48,256]{1,0:T(8,128)S(1)} %get-tuple-element.66), channel_id=1, source_target_pairs={{0,24},{4,28},{8,16},{12,20},{16,8},{20,12},{24,0},{28,4},{1,25},{... | collective-permute-start | bytes 147464 | tf_op jit(solution)/shard_map/ppermute | solution.py:402
  64.1 6.0 %collective-permute-start.16 = (f32[48,256]{1,0:T(8,128)S(1)}, f32[48,256]{1,0:T(8,128)S(1)}, u32[]{:S(2)}, u32[]{:S(2)}) collective-permute-start(f32[48,256]{1,0:T(8,128)S(1)} %add_add_fusion.refs_0_), channel_id=1, source_target_pairs={{0,3},{1,2},{2,1},{3,0},{4,7},{5,6},{6,5},{7,4},{8,11},{9,10},{10,... | collective-permute-start | bytes 147464 | tf_op jit(solution)/shard_map/ppermute | solution.py:402
  65.6 5.0 %collective-permute-start.15 = (f32[48,256]{1,0:T(8,128)S(1)}, f32[48,256]{1,0:T(8,128)S(1)}, u32[]{:S(2)}, u32[]{:S(2)}) collective-permute-start(f32[48,256]{1,0:T(8,128)S(1)} %add_add_fusion.refs_0_), channel_id=1, source_target_pairs={{0,2},{1,3},{2,0},{3,1},{4,6},{5,7},{6,4},{7,5},{8,10},{9,11},{10,... | collective-permute-start | bytes 147464 | tf_op jit(solution)/shard_map/ppermute | solution.py:402
  66.5 4.6 %collective-permute-start.14 = (f32[48,256]{1,0:T(8,128)S(1)}, f32[48,256]{1,0:T(8,128)S(1)}, u32[]{:S(2)}, u32[]{:S(2)}) collective-permute-start(f32[48,256]{1,0:T(8,128)S(1)} %add_add_fusion.refs_0_), channel_id=1, source_target_pairs={{0,1},{1,0},{2,3},{3,2},{4,5},{5,4},{6,7},{7,6},{8,9},{9,8},{10,11... | collective-permute-start | bytes 147464 | tf_op jit(solution)/shard_map/ppermute | solution.py:402

commit v4 on v3

--- a/solution.py
+++ b/solution.py
@@ -434,7 +434,7 @@
     mine, other = gather(member, aligned, squares, "pairs", "frames", comps)
     sums = merge(mine, swap(other, "frames", 1))
     total = sums[0]
-    for s in range(1, len(sums)):
+    for s in reversed(range(1, len(sums))):
         total = total + swap(sums[s], "frames", 2 * s)
     new_centroids, occupancy = update(centroids, gathered(total, "pairs"), "pairs", quarter)
     return (tica.T, jnp.transpose(new_centroids, (1, 0, 2)), occupancy[0])

time: 72.2 us -> 71.2 us (0.986)
  waiting for transfers between devices: 13 us -> 12 us
    ppermute x17, waiting for transfers between devices: 13 us -> 12 us  [swap(): return lax.ppermute(value, axis, [(i, i ^ step) for i in range(size)])]
  transfers between devices with their start and end apart: 17 -> 17, of which waited for: 10 -> 10; matrix products, arithmetic and copies ran while one was open for 0% -> 0% of each run, Pallas kernels for 45% -> 46%
where the time goes in v4:
time: 71.2 us; the launch traced here: 71.1 us
  Pallas kernels  34.6 us (49%)
  starting transfers between devices  21.9 us (31%)
  waiting for transfers between devices  12 us (17%)
  local copies, waits for them, and re-layouts  1.69 us (2%)
  between operations  0.78 us (1%)
    pallas_call x1, Pallas kernels, project(): pl.pallas_call(functools.partial(project_kernel, axis, share, res_count),...  27.8 us
    ppermute x17, starting transfers between devices, swap(): return lax.ppermute(value, axis, [(i, i ^ step) for i in range(size)])  21.9 us
    ppermute x17, waiting for transfers between devices, swap(): return lax.ppermute(value, axis, [(i, i ^ step) for i in range(size)])  12 us
    pallas_call x1, Pallas kernels, align(): pl.pallas_call(functools.partial(align_kernel, frames_axis, pairs_axis, q...  3.09 us
    unnamed x16, local copies, waits for them, and re-layouts  1.69 us
    pallas_call x1, Pallas kernels, split_coords(): pl.pallas_call(split_kernel, out_shape=[jax.ShapeDtypeStruct((dims * fram...  1.55 us
  transfers between devices with their start and end apart: 17, of which 10 were waited for; matrix products, arithmetic and copies ran while one was open for 0% of the time, Pallas kernels for 46%

profile of v4, /device:TPU:0, one launch (start us, length us, event | category | flops | bytes accessed | tf_op | source)
XLA Modules:
  0.0 71.1 jit_solution(17530378477453028736)
XLA Ops:
  0.6 0.5 collective-permute-start
  1.2 1.7 %copy-done.2 = f32[640,3,300]{0,2,1:T(8,128)S(1)} copy-done((f32[640,3,300]{0,2,1:T(8,128)S(1)}, f32[640,3,300]{0,2,1:T(8,128)}, u32[]{:S(2)}) %copy-start.2) | copy-done | bytes 2304024
  2.8 1.6 %split.1 = (f8e4m3fn[1920,1024]{1,0:T(32,128)(4,1)S(1)}, f32[640,128]{1,0:T(8,128)S(1)}) custom-call(f32[3,300,640]{2,1,0:T(8,128)S(1)} %bitcast.14), custom_call_target="tpu_custom_call" | custom-call | flops 1073741824 | bytes 8388608 | tf_op jit(solution)/shard_map/split/pallas_call | solution.py:73
  4.4 3.6 %collective-permute-start.3 = (f32[2,3,48,300]{3,2,1,0:T(8,128)S(1)}, f32[2,3,48,300]{3,2,1,0:T(8,128)S(1)}, u32[]{:S(2)}, u32[]{:S(2)}) collective-permute-start(f32[2,3,48,300]{3,2,1,0:T(8,128)S(1)} %pad_maximum_fusion.refs_0_), channel_id=1, source_target_pairs={{0,24},{4,28},{8,16},{12,20},{16,8},{20,12},{24,0},{28,4},{1,25},{... | collective-permute-start | bytes 1036808 | tf_op jit(solution)/shard_map/ppermute | solution.py:402
  8.0 0.5 collective-permute-start.2
  8.5 0.1 collective-permute-start.1
  8.7 27.8 %project.1 = (f32[125,128]{1,0:T(8,128)S(1)}, f32[125,128]{1,0:T(8,128)S(1)}, f32[125,128]{1,0:T(8,128)S(1)}, f32[125,128]{1,0:T(8,128)S(1)}) custom-call(s32[2,11264]{1,0:T(2,128)S(1)} %copy-done.4, f32[1,11264]{1,0:T(1,128)S(1)} %bitcast.16, bf16[100,11264]{1,0:T(8,128)(2,1)S(1)} %bitcast.13, f8e4m3fn[1920,1024]{1,0:T(32,128)(4,1)S(1)} %get-tuple-element.37.positions_ref, ...), custom_call_target="tpu_custom_call" | custom-call | flops 44291850240 | bytes 8388608 | tf_op jit(solution)/shard_map/project/pallas_call | solution.py:157
  36.6 4.1 %collective-permute-start.4 = (f32[125,128]{1,0:T(8,128)S(1)}, f32[125,128]{1,0:T(8,128)S(1)}, u32[]{:S(2)}, u32[]{:S(2)}) collective-permute-start(f32[125,128]{1,0:T(8,128)S(1)} %get-tuple-element.51), channel_id=1, source_target_pairs={{0,3},{1,2},{2,1},{3,0},{4,7},{5,6},{6,5},{7,4},{8,11},{9,10},{10,... | collective-permute-start | bytes 192008 | tf_op jit(solution)/shard_map/ppermute | solution.py:402
  40.6 0.6 collective-permute-start.6
  41.3 3.1 %align.1 = (bf16[384,640]{1,0:T(8,128)(2,1)S(1)}, f32[240,640]{1,0:T(8,128)S(1)}) custom-call(f32[3,300,640]{2,1,0:T(8,128)S(1)} %bitcast.15, s32[640]{0:T(1024)S(1)} %copy-done.6, s32[384]{0:T(512)S(1)} %copy-done.7, f32[2,3,48,300]{3,2,1,0:T(8,128)S(1)} %pad_maximum_fusion.refs_0_, f32[2,3,48,300]{3,2,1,0:T(8,128)S(1)} %collective-permute-done.1.refs_1_, ...), custom_call_target="tpu_custom_call" | custom-call | flops 1769472000 | bytes 4194304 | tf_op jit(solution)/shard_map/align/pallas_call | solution.py:284
  44.4 1.6 %collective-permute-done.5.refs_2_ = f32[125,128]{1,0:T(8,128)S(1)} collective-permute-done((f32[125,128]{1,0:T(8,128)S(1)}, f32[125,128]{1,0:T(8,128)S(1)}, u32[]{:S(2)}, u32[]{:S(2)}) %collective-permute-start.5) | collective-permute-done | bytes 64032 | tf_op jit(solution)/shard_map/ppermute | solution.py:402
  46.0 0.7 finish.1
  46.7 2.7 %collective-permute-start.9 = (f32[1,640]{1,0:T(1,128)S(1)}, f32[1,640]{1,0:T(1,128)S(1)}, u32[]{:S(2)}, u32[]{:S(2)}) collective-permute-start(f32[1,640]{1,0:T(1,128)S(1)} %get-tuple-element.60.refs_0_), channel_id=1, source_target_pairs={{0,3},{1,2},{2,1},{3,0},{4,7},{5,6},{6,5},{7,4},{8,11},{9,10},{10,... | collective-permute-start | bytes 7688 | tf_op jit(solution)/shard_map/ppermute | solution.py:402
  49.4 1.7 %collective-permute-start.7 = (f32[1,640]{1,0:T(1,128)S(1)}, f32[1,640]{1,0:T(1,128)S(1)}, u32[]{:S(2)}, u32[]{:S(2)}) collective-permute-start(f32[1,640]{1,0:T(1,128)S(1)} %get-tuple-element.60.refs_0_), channel_id=1, source_target_pairs={{0,1},{1,0},{2,3},{3,2},{4,5},{5,4},{6,7},{7,6},{8,9},{9,8},{10,11... | collective-permute-start | bytes 7688 | tf_op jit(solution)/shard_map/ppermute | solution.py:402
  51.1 1.0 %collective-permute-done.9.refs_3_ = f32[1,640]{1,0:T(1,128)S(1)} collective-permute-done((f32[1,640]{1,0:T(1,128)S(1)}, f32[1,640]{1,0:T(1,128)S(1)}, u32[]{:S(2)}, u32[]{:S(2)}) %collective-permute-start.9) | collective-permute-done | bytes 2592 | tf_op jit(solution)/shard_map/ppermute | solution.py:402
  52.1 1.8 %collective-permute-done.8.refs_2_ = f32[1,640]{1,0:T(1,128)S(1)} collective-permute-done((f32[1,640]{1,0:T(1,128)S(1)}, f32[1,640]{1,0:T(1,128)S(1)}, u32[]{:S(2)}, u32[]{:S(2)}) %collective-permute-start.8) | collective-permute-done | bytes 2592 | tf_op jit(solution)/shard_map/ppermute | solution.py:402
  53.9 0.5 gather.1
  54.4 0.1 collective-permute-start.10
  54.5 1.4 %collective-permute-done.10.other_ref = f32[4,48,256]{2,1,0:T(8,128)S(1)} collective-permute-done((f32[4,48,256]{2,1,0:T(8,128)S(1)}, f32[4,48,256]{2,1,0:T(8,128)S(1)}, u32[]{:S(2)}, u32[]{:S(2)}) %collective-permute-start.10) | collective-permute-done | bytes 196640 | tf_op jit(solution)/shard_map/ppermute | solution.py:402
  56.0 2.5 %collective-permute-start.11 = (f32[48,256]{1,0:T(8,128)S(1)}, f32[48,256]{1,0:T(8,128)S(1)}, u32[]{:S(2)}, u32[]{:S(2)}) collective-permute-start(f32[48,256]{1,0:T(8,128)S(1)} %get-tuple-element.64), channel_id=1, source_target_pairs={{0,24},{4,28},{8,16},{12,20},{16,8},{20,12},{24,0},{28,4},{1,25},{... | collective-permute-start | bytes 147464 | tf_op jit(solution)/shard_map/ppermute | solution.py:402
  58.5 0.5 collective-permute-start.12
  59.0 0.5 collective-permute-start.13
  59.5 1.5 %collective-permute-done.11 = f32[48,256]{1,0:T(8,128)S(1)} collective-permute-done((f32[48,256]{1,0:T(8,128)S(1)}, f32[48,256]{1,0:T(8,128)S(1)}, u32[]{:S(2)}, u32[]{:S(2)}) %collective-permute-start.11) | collective-permute-done | bytes 49184 | tf_op jit(solution)/shard_map/ppermute | solution.py:402
  61.0 1.5 %collective-permute-done.12 = f32[48,256]{1,0:T(8,128)S(1)} collective-permute-done((f32[48,256]{1,0:T(8,128)S(1)}, f32[48,256]{1,0:T(8,128)S(1)}, u32[]{:S(2)}, u32[]{:S(2)}) %collective-permute-start.12) | collective-permute-done | bytes 49184 | tf_op jit(solution)/shard_map/ppermute | solution.py:402
  62.6 0.5 collective-permute-done.13
  63.1 1.5 %collective-permute-start.16 = (f32[48,256]{1,0:T(8,128)S(1)}, f32[48,256]{1,0:T(8,128)S(1)}, u32[]{:S(2)}, u32[]{:S(2)}) collective-permute-start(f32[48,256]{1,0:T(8,128)S(1)} %add_add_fusion.refs_0_), channel_id=1, source_target_pairs={{0,3},{1,2},{2,1},{3,0},{4,7},{5,6},{6,5},{7,4},{8,11},{9,10},{10,... | collective-permute-start | bytes 147464 | tf_op jit(solution)/shard_map/ppermute | solution.py:402
  64.6 0.9 %collective-permute-start.15 = (f32[48,256]{1,0:T(8,128)S(1)}, f32[48,256]{1,0:T(8,128)S(1)}, u32[]{:S(2)}, u32[]{:S(2)}) collective-permute-start(f32[48,256]{1,0:T(8,128)S(1)} %add_add_fusion.refs_0_), channel_id=1, source_target_pairs={{0,2},{1,3},{2,0},{3,1},{4,6},{5,7},{6,4},{7,5},{8,10},{9,11},{10,... | collective-permute-start | bytes 147464 | tf_op jit(solution)/shard_map/ppermute | solution.py:402
  65.5 2.0 %collective-permute-start.14 = (f32[48,256]{1,0:T(8,128)S(1)}, f32[48,256]{1,0:T(8,128)S(1)}, u32[]{:S(2)}, u32[]{:S(2)}) collective-permute-start(f32[48,256]{1,0:T(8,128)S(1)} %add_add_fusion.refs_0_), channel_id=1, source_target_pairs={{0,1},{1,0},{2,3},{3,2},{4,5},{5,4},{6,7},{7,6},{8,9},{9,8},{10,11... | collective-permute-start | bytes 147464 | tf_op jit(solution)/shard_map/ppermute | solution.py:402
  67.6 1.5 %collective-permute-done.16.refs_3_ = f32[48,256]{1,0:T(8,128)S(1)} collective-permute-done((f32[48,256]{1,0:T(8,128)S(1)}, f32[48,256]{1,0:T(8,128)S(1)}, u32[]{:S(2)}, u32[]{:S(2)}) %collective-permute-start.16) | collective-permute-done | bytes 49184 | tf_op jit(solution)/shard_map/ppermute | solution.py:402
  69.1 0.6 collective-permute-done.15.refs_2_
  69.7 0.5 collective-permute-done.14.refs_1_
  70.1 0.9 %update.1 = (f32[3,48,300]{2,1,0:T(8,128)}, f32[1,48]{1,0:T(1,128)}) custom-call(f32[3,48,300]{2,1,0:T(8,128)S(1)} %bitcast.12, f32[48,256]{1,0:T(8,128)S(1)} %add_add_fusion.refs_0_, f32[48,256]{1,0:T(8,128)S(1)} %collective-permute-done.14.refs_1_, f32[48,256]{1,0:T(8,128)S(1)} %collective-permute-done.15.refs_2_, ...), custom_call_target="tpu_custom_call" | custom-call | tf_op jit(solution)/shard_map/update/pallas_call | solution.py:388
  (27 shorter events, 0.1 us)
Async XLA Ops:
  0.6 3.8 %copy-start = (f32[48,3,300]{2,0,1:T(8,128)S(1)}, f32[48,3,300]{2,0,1:T(8,128)}, u32[]{:S(2)}) copy-start(f32[48,3,300]{2,0,1:T(8,128)} %param.8) | copy-start | bytes 518404
  0.6 3.7 %collective-permute-start = (f32[3,48,300]{2,1,0:T(8,128)}, f32[3,48,300]{2,1,0:T(8,128)S(1)}, u32[]{:S(2)}, u32[]{:S(2)}) collective-permute-start(f32[3,48,300]{2,1,0:T(8,128)} %bitcast.10), channel_id=1, source_target_pairs={{0,4},{4,0},{8,12},{12,8},{16,20},{20,16},{24,28},{28,24},{1,5},{5... | collective-permute-start | bytes 518408 | tf_op jit(solution)/shard_map/ppermute | solution.py:402
  1.2 1.7 %copy-start.2 = (f32[640,3,300]{0,2,1:T(8,128)S(1)}, f32[640,3,300]{0,2,1:T(8,128)}, u32[]{:S(2)}) copy-start(f32[640,3,300]{0,2,1:T(8,128)} %param.7) | copy-start | bytes 6912004
  2.8 5.8 %copy-start.1 = (bf16[11264,100]{0,1:T(8,128)(2,1)S(1)}, bf16[11264,100]{0,1:T(8,128)(2,1)}, u32[]{:S(2)}) copy-start(bf16[11264,100]{0,1:T(8,128)(2,1)} %param.13) | copy-start | bytes 6758404
  2.8 5.8 %copy-start.4 = (s32[2,11264]{1,0:T(2,128)S(1)}, s32[2,11264]{1,0:T(2,128)}, u32[]{:S(2)}) copy-start(s32[2,11264]{1,0:T(2,128)} %index_ref.1) | copy-start | bytes 270340
  2.8 5.8 %copy-start.5 = (f32[11264]{0:T(1024)S(1)}, f32[11264]{0:T(1024)}, u32[]{:S(2)}) copy-start(f32[11264]{0:T(1024)} %param.12) | copy-start | bytes 135172
  4.4 32.1 %collective-permute-start.3 = (f32[2,3,48,300]{3,2,1,0:T(8,128)S(1)}, f32[2,3,48,300]{3,2,1,0:T(8,128)S(1)}, u32[]{:S(2)}, u32[]{:S(2)}) collective-permute-start(f32[2,3,48,300]{3,2,1,0:T(8,128)S(1)} %pad_maximum_fusion.refs_0_), channel_id=1, source_target_pairs={{0,24},{4,28},{8,16},{12,20},{16,8},{20,12},{24,0},{28,4},{1,25},{... | collective-permute-start | bytes 1036808 | tf_op jit(solution)/shard_map/ppermute | solution.py:402
  8.0 28.5 %collective-permute-start.2 = (f32[2,3,48,300]{3,2,1,0:T(8,128)S(1)}, f32[2,3,48,300]{3,2,1,0:T(8,128)S(1)}, u32[]{:S(2)}, u32[]{:S(2)}) collective-permute-start(f32[2,3,48,300]{3,2,1,0:T(8,128)S(1)} %pad_maximum_fusion.refs_0_), channel_id=1, source_target_pairs={{0,16},{4,20},{8,24},{12,28},{16,0},{20,4},{24,8},{28,12},{1,17},{... | collective-permute-start | bytes 1036808 | tf_op jit(solution)/shard_map/ppermute | solution.py:402
  8.5 28.0 %collective-permute-start.1 = (f32[2,3,48,300]{3,2,1,0:T(8,128)S(1)}, f32[2,3,48,300]{3,2,1,0:T(8,128)S(1)}, u32[]{:S(2)}, u32[]{:S(2)}) collective-permute-start(f32[2,3,48,300]{3,2,1,0:T(8,128)S(1)} %pad_maximum_fusion.refs_0_), channel_id=1, source_target_pairs={{0,8},{4,12},{8,0},{12,4},{16,24},{20,28},{24,16},{28,20},{1,9},{5... | collective-permute-start | bytes 1036808 | tf_op jit(solution)/shard_map/ppermute | solution.py:402
  8.6 32.6 %copy-start.3 = (f32[640,3,300]{0,2,1:T(8,128)S(1)}, f32[640,3,300]{0,2,1:T(8,128)}, u32[]{:S(2)}) copy-start(f32[640,3,300]{0,2,1:T(8,128)} %param.7) | copy-start | bytes 6912004
  8.7 32.6 %copy-start.6 = (s32[640]{0:T(1024)S(1)}, s32[640]{0:T(1024)}, u32[]{:S(2)}) copy-start(s32[640]{0:T(1024)} %assigned_ref.1) | copy-start | bytes 7684
  8.7 32.6 %copy-start.7 = (s32[384]{0:T(512)S(1)}, s32[384]{0:T(512)}, u32[]{:S(2)}) copy-start(s32[384]{0:T(512)} %home_ref.1) | copy-start | bytes 4612
  36.6 7.8 %collective-permute-start.4 = (f32[125,128]{1,0:T(8,128)S(1)}, f32[125,128]{1,0:T(8,128)S(1)}, u32[]{:S(2)}, u32[]{:S(2)}) collective-permute-start(f32[125,128]{1,0:T(8,128)S(1)} %get-tuple-element.51), channel_id=1, source_target_pairs={{0,3},{1,2},{2,1},{3,0},{4,7},{5,6},{6,5},{7,4},{8,11},{9,10},{10,... | collective-permute-start | bytes 192008 | tf_op jit(solution)/shard_map/ppermute | solution.py:402
  40.6 5.4 %collective-permute-start.5 = (f32[125,128]{1,0:T(8,128)S(1)}, f32[125,128]{1,0:T(8,128)S(1)}, u32[]{:S(2)}, u32[]{:S(2)}) collective-permute-start(f32[125,128]{1,0:T(8,128)S(1)} %get-tuple-element.52), channel_id=1, source_target_pairs={{0,2},{1,3},{2,0},{3,1},{4,6},{5,7},{6,4},{7,5},{8,10},{9,11},{10,... | collective-permute-start | bytes 192008 | tf_op jit(solution)/shard_map/ppermute | solution.py:402
  40.6 5.4 %collective-permute-start.6 = (f32[125,128]{1,0:T(8,128)S(1)}, f32[125,128]{1,0:T(8,128)S(1)}, u32[]{:S(2)}, u32[]{:S(2)}) collective-permute-start(f32[125,128]{1,0:T(8,128)S(1)} %get-tuple-element.53), channel_id=1, source_target_pairs={{0,1},{1,0},{2,3},{3,2},{4,5},{5,4},{6,7},{7,6},{8,9},{9,8},{10,11... | collective-permute-start | bytes 192008 | tf_op jit(solution)/shard_map/ppermute | solution.py:402
  46.7 5.4 %collective-permute-start.9 = (f32[1,640]{1,0:T(1,128)S(1)}, f32[1,640]{1,0:T(1,128)S(1)}, u32[]{:S(2)}, u32[]{:S(2)}) collective-permute-start(f32[1,640]{1,0:T(1,128)S(1)} %get-tuple-element.60.refs_0_), channel_id=1, source_target_pairs={{0,3},{1,2},{2,1},{3,0},{4,7},{5,6},{6,5},{7,4},{8,11},{9,10},{10,... | collective-permute-start | bytes 7688 | tf_op jit(solution)/shard_map/ppermute | solution.py:402
  49.4 4.5 %collective-permute-start.8 = (f32[1,640]{1,0:T(1,128)S(1)}, f32[1,640]{1,0:T(1,128)S(1)}, u32[]{:S(2)}, u32[]{:S(2)}) collective-permute-start(f32[1,640]{1,0:T(1,128)S(1)} %get-tuple-element.60.refs_0_), channel_id=1, source_target_pairs={{0,2},{1,3},{2,0},{3,1},{4,6},{5,7},{6,4},{7,5},{8,10},{9,11},{10,... | collective-permute-start | bytes 7688 | tf_op jit(solution)/shard_map/ppermute | solution.py:402
  49.4 4.5 %collective-permute-start.7 = (f32[1,640]{1,0:T(1,128)S(1)}, f32[1,640]{1,0:T(1,128)S(1)}, u32[]{:S(2)}, u32[]{:S(2)}) collective-permute-start(f32[1,640]{1,0:T(1,128)S(1)} %get-tuple-element.60.refs_0_), channel_id=1, source_target_pairs={{0,1},{1,0},{2,3},{3,2},{4,5},{5,4},{6,7},{7,6},{8,9},{9,8},{10,11... | collective-permute-start | bytes 7688 | tf_op jit(solution)/shard_map/ppermute | solution.py:402
  54.4 1.5 %collective-permute-start.10 = (f32[4,48,256]{2,1,0:T(8,128)S(1)}, f32[4,48,256]{2,1,0:T(8,128)S(1)}, u32[]{:S(2)}, u32[]{:S(2)}) collective-permute-start(f32[4,48,256]{2,1,0:T(8,128)S(1)} %get-tuple-element.62), channel_id=1, source_target_pairs={{0,4},{4,0},{8,12},{12,8},{16,20},{20,16},{24,28},{28,24},{1,5},{5... | collective-permute-start | bytes 589832 | tf_op jit(solution)/shard_map/ppermute | solution.py:402
  56.0 5.1 %collective-permute-start.11 = (f32[48,256]{1,0:T(8,128)S(1)}, f32[48,256]{1,0:T(8,128)S(1)}, u32[]{:S(2)}, u32[]{:S(2)}) collective-permute-start(f32[48,256]{1,0:T(8,128)S(1)} %get-tuple-element.64), channel_id=1, source_target_pairs={{0,24},{4,28},{8,16},{12,20},{16,8},{20,12},{24,0},{28,4},{1,25},{... | collective-permute-start | bytes 147464 | tf_op jit(solution)/shard_map/ppermute | solution.py:402
  58.5 4.1 %collective-permute-start.12 = (f32[48,256]{1,0:T(8,128)S(1)}, f32[48,256]{1,0:T(8,128)S(1)}, u32[]{:S(2)}, u32[]{:S(2)}) collective-permute-start(f32[48,256]{1,0:T(8,128)S(1)} %get-tuple-element.65), channel_id=1, source_target_pairs={{0,16},{4,20},{8,24},{12,28},{16,0},{20,4},{24,8},{28,12},{1,17},{... | collective-permute-start | bytes 147464 | tf_op jit(solution)/shard_map/ppermute | solution.py:402
  59.0 4.1 %collective-permute-start.13 = (f32[48,256]{1,0:T(8,128)S(1)}, f32[48,256]{1,0:T(8,128)S(1)}, u32[]{:S(2)}, u32[]{:S(2)}) collective-permute-start(f32[48,256]{1,0:T(8,128)S(1)} %get-tuple-element.66), channel_id=1, source_target_pairs={{0,8},{4,12},{8,0},{12,4},{16,24},{20,28},{24,16},{28,20},{1,9},{5... | collective-permute-start | bytes 147464 | tf_op jit(solution)/shard_map/ppermute | solution.py:402
  63.1 6.0 %collective-permute-start.16 = (f32[48,256]{1,0:T(8,128)S(1)}, f32[48,256]{1,0:T(8,128)S(1)}, u32[]{:S(2)}, u32[]{:S(2)}) collective-permute-start(f32[48,256]{1,0:T(8,128)S(1)} %add_add_fusion.refs_0_), channel_id=1, source_target_pairs={{0,3},{1,2},{2,1},{3,0},{4,7},{5,6},{6,5},{7,4},{8,11},{9,10},{10,... | collective-permute-start | bytes 147464 | tf_op jit(solution)/shard_map/ppermute | solution.py:402
  64.6 5.0 %collective-permute-start.15 = (f32[48,256]{1,0:T(8,128)S(1)}, f32[48,256]{1,0:T(8,128)S(1)}, u32[]{:S(2)}, u32[]{:S(2)}) collective-permute-start(f32[48,256]{1,0:T(8,128)S(1)} %add_add_fusion.refs_0_), channel_id=1, source_target_pairs={{0,2},{1,3},{2,0},{3,1},{4,6},{5,7},{6,4},{7,5},{8,10},{9,11},{10,... | collective-permute-start | bytes 147464 | tf_op jit(solution)/shard_map/ppermute | solution.py:402
  65.5 4.6 %collective-permute-start.14 = (f32[48,256]{1,0:T(8,128)S(1)}, f32[48,256]{1,0:T(8,128)S(1)}, u32[]{:S(2)}, u32[]{:S(2)}) collective-permute-start(f32[48,256]{1,0:T(8,128)S(1)} %add_add_fusion.refs_0_), channel_id=1, source_target_pairs={{0,1},{1,0},{2,3},{3,2},{4,5},{5,4},{6,7},{7,6},{8,9},{9,8},{10,11... | collective-permute-start | bytes 147464 | tf_op jit(solution)/shard_map/ppermute | solution.py:402

commit v5 on v4

--- a/solution.py
+++ b/solution.py
@@ -45,7 +45,8 @@
     reach = jnp.maximum(reach, 1e-30)
     unit_ref[...] = jnp.broadcast_to(reach * (1.0 / REACH), (128, frames)).T
     scale = REACH / reach
-    rows_ref[res_count:, :] = jnp.zeros((rows_ref.shape[0] - res_count, frames), jnp.float32)
+    below = res_count // 8 * 8
+    rows_ref[below:, :] = jnp.zeros((rows_ref.shape[0] - below, frames), jnp.float32)
     lane = lax.broadcasted_iota(jnp.int32, (frames, LANES), 1)
     for c in range(dims):
         rows_ref[0:res_count, :] = centered[c] * scale
@@ -143,8 +144,11 @@
             value = rows[0]
             for k in range(1, parts):
                 value = jnp.where(me ^ s == k, rows[k], value)
-            for j in range(frames // LANES):
-                out_ref[j * share : (j + 1) * share, :] = value[:, j * LANES : (j + 1) * LANES]
+            packed = [value[:, j * LANES : (j + 1) * LANES] for j in range(frames // LANES)]
+            spare = out_ref.shape[0] - len(packed) * share
+            if spare:
+                packed.append(jnp.zeros((spare, LANES), jnp.float32))
+            out_ref[...] = jnp.concatenate(packed, axis=0)
 
 
 def project(positions, unit, res_count, pair_index, mean_dist, tica_weight, axis):
@@ -152,6 +156,7 @@
     comps, pairs = tica_weight.shape
     parts = lax.axis_size(axis)
     share = comps // parts
+    packed = round_up(share * frames // LANES, 8)
     block = next(b for b in (2816, 1408, 1024, 512, 256, 128, pairs) if pairs % b == 0)
     depth = positions.shape[1]
     return pl.pallas_call(
@@ -164,8 +169,8 @@
             pl.BlockSpec(positions.shape, lambda i: (0, 0)),
             pl.BlockSpec(unit.shape, lambda i: (0, 0)),
         ],
-        out_specs=[pl.BlockSpec((share * frames // LANES, LANES), lambda i: (0, 0))] * parts,
-        out_shape=[jax.ShapeDtypeStruct((share * frames // LANES, LANES), jnp.float32)] * parts,
+        out_specs=[pl.BlockSpec((packed, LANES), lambda i: (0, 0))] * parts,
+        out_shape=[jax.ShapeDtypeStruct((packed, LANES), jnp.float32)] * parts,
         scratch_shapes=[
             pltpu.VMEM((depth, block), piece_type),
             pltpu.VMEM((frames, round_up(comps, 128)), jnp.float32),
@@ -190,8 +195,7 @@
         square_ref[:, j * LANES : (j + 1) * LANES] = jnp.sum(part * part, axis=0, keepdims=True)
 
 
-def finish(partial, frames):
-    share = partial[0].size // frames
+def finish(partial, share, frames):
     return pl.pallas_call(
         finish_kernel,
         out_shape=[
@@ -429,7 +433,7 @@
             received,
         )
     )
-    tica, square = finish([partial[0], *received], coords.shape[2])
+    tica, square = finish([partial[0], *received], comps // parts, coords.shape[2])
     squares = gathered(square, "pairs")
     mine, other = gather(member, aligned, squares, "pairs", "frames", comps)
     sums = merge(mine, swap(other, "frames", 1))

time: 71.2 us -> 71.3 us (level)
  no operation moved by 1% of the time
where the time goes in v5:
time: 71.3 us; the launch traced here: 71.1 us
  Pallas kernels  34.7 us (49%)
  starting transfers between devices  21.9 us (31%)
  waiting for transfers between devices  12 us (17%)
  local copies, waits for them, and re-layouts  1.69 us (2%)
  between operations  0.78 us (1%)
    pallas_call x1, Pallas kernels, project(): pl.pallas_call(functools.partial(project_kernel, axis, share, res_count),...  27.9 us
    ppermute x17, starting transfers between devices, swap(): return lax.ppermute(value, axis, [(i, i ^ step) for i in range(size)])  21.9 us
    ppermute x17, waiting for transfers between devices, swap(): return lax.ppermute(value, axis, [(i, i ^ step) for i in range(size)])  12 us
    pallas_call x1, Pallas kernels, align(): pl.pallas_call(functools.partial(align_kernel, frames_axis, pairs_axis, q...  3.09 us
    unnamed x16, local copies, waits for them, and re-layouts  1.69 us
    pallas_call x1, Pallas kernels, split_coords(): pl.pallas_call(split_kernel, out_shape=[jax.ShapeDtypeStruct((dims * fram...  1.55 us
  transfers between devices with their start and end apart: 17, of which 10 were waited for; matrix products, arithmetic and copies ran while one was open for 0% of the time, Pallas kernels for 46%

profile of v5, /device:TPU:0, one launch (start us, length us, event | category | flops | bytes accessed | tf_op | source)
XLA Modules:
  0.0 71.1 jit_solution(7295758114654076066)
XLA Ops:
  0.6 0.5 collective-permute-start
  1.2 1.7 %copy-done.2 = f32[640,3,300]{0,2,1:T(8,128)S(1)} copy-done((f32[640,3,300]{0,2,1:T(8,128)S(1)}, f32[640,3,300]{0,2,1:T(8,128)}, u32[]{:S(2)}) %copy-start.2) | copy-done | bytes 2304024
  2.8 1.6 %split.1 = (f8e4m3fn[1920,1024]{1,0:T(32,128)(4,1)S(1)}, f32[640,128]{1,0:T(8,128)S(1)}) custom-call(f32[3,300,640]{2,1,0:T(8,128)S(1)} %bitcast.14), custom_call_target="tpu_custom_call" | custom-call | flops 1073741824 | bytes 8388608 | tf_op jit(solution)/shard_map/split/pallas_call | solution.py:74
  4.4 3.6 %collective-permute-start.3 = (f32[2,3,48,300]{3,2,1,0:T(8,128)S(1)}, f32[2,3,48,300]{3,2,1,0:T(8,128)S(1)}, u32[]{:S(2)}, u32[]{:S(2)}) collective-permute-start(f32[2,3,48,300]{3,2,1,0:T(8,128)S(1)} %pad_maximum_fusion.refs_0_), channel_id=1, source_target_pairs={{0,24},{4,28},{8,16},{12,20},{16,8},{20,12},{24,0},{28,4},{1,25},{... | collective-permute-start | bytes 1036808 | tf_op jit(solution)/shard_map/ppermute | solution.py:406
  8.0 0.5 collective-permute-start.2
  8.5 0.1 collective-permute-start.1
  8.7 27.9 %project.1 = (f32[128,128]{1,0:T(8,128)S(1)}, f32[128,128]{1,0:T(8,128)S(1)}, f32[128,128]{1,0:T(8,128)S(1)}, f32[128,128]{1,0:T(8,128)S(1)}) custom-call(s32[2,11264]{1,0:T(2,128)S(1)} %copy-done.4, f32[1,11264]{1,0:T(1,128)S(1)} %bitcast.16, bf16[100,11264]{1,0:T(8,128)(2,1)S(1)} %bitcast.13, f8e4m3fn[1920,1024]{1,0:T(32,128)(4,1)S(1)} %get-tuple-element.37.positions_ref, ...), custom_call_target="tpu_custom_call" | custom-call | flops 44291850240 | bytes 8388608 | tf_op jit(solution)/shard_map/project/pallas_call | solution.py:162
  36.6 4.1 %collective-permute-start.4 = (f32[128,128]{1,0:T(8,128)S(1)}, f32[128,128]{1,0:T(8,128)S(1)}, u32[]{:S(2)}, u32[]{:S(2)}) collective-permute-start(f32[128,128]{1,0:T(8,128)S(1)} %get-tuple-element.51), channel_id=1, source_target_pairs={{0,3},{1,2},{2,1},{3,0},{4,7},{5,6},{6,5},{7,4},{8,11},{9,10},{10,... | collective-permute-start | bytes 196616 | tf_op jit(solution)/shard_map/ppermute | solution.py:406
  40.6 0.6 collective-permute-start.6
  41.3 3.1 %align.1 = (bf16[384,640]{1,0:T(8,128)(2,1)S(1)}, f32[240,640]{1,0:T(8,128)S(1)}) custom-call(f32[3,300,640]{2,1,0:T(8,128)S(1)} %bitcast.15, s32[640]{0:T(1024)S(1)} %copy-done.6, s32[384]{0:T(512)S(1)} %copy-done.7, f32[2,3,48,300]{3,2,1,0:T(8,128)S(1)} %pad_maximum_fusion.refs_0_, f32[2,3,48,300]{3,2,1,0:T(8,128)S(1)} %collective-permute-done.1.refs_1_, ...), custom_call_target="tpu_custom_call" | custom-call | flops 1769472000 | bytes 4194304 | tf_op jit(solution)/shard_map/align/pallas_call | solution.py:288
  44.4 1.7 %collective-permute-done.5.refs_2_ = f32[128,128]{1,0:T(8,128)S(1)} collective-permute-done((f32[128,128]{1,0:T(8,128)S(1)}, f32[128,128]{1,0:T(8,128)S(1)}, u32[]{:S(2)}, u32[]{:S(2)}) %collective-permute-start.5) | collective-permute-done | bytes 65568 | tf_op jit(solution)/shard_map/ppermute | solution.py:406
  46.1 0.7 finish.1
  46.7 2.7 %collective-permute-start.9 = (f32[1,640]{1,0:T(1,128)S(1)}, f32[1,640]{1,0:T(1,128)S(1)}, u32[]{:S(2)}, u32[]{:S(2)}) collective-permute-start(f32[1,640]{1,0:T(1,128)S(1)} %get-tuple-element.60.refs_0_), channel_id=1, source_target_pairs={{0,3},{1,2},{2,1},{3,0},{4,7},{5,6},{6,5},{7,4},{8,11},{9,10},{10,... | collective-permute-start | bytes 7688 | tf_op jit(solution)/shard_map/ppermute | solution.py:406
  49.4 1.7 %collective-permute-start.7 = (f32[1,640]{1,0:T(1,128)S(1)}, f32[1,640]{1,0:T(1,128)S(1)}, u32[]{:S(2)}, u32[]{:S(2)}) collective-permute-start(f32[1,640]{1,0:T(1,128)S(1)} %get-tuple-element.60.refs_0_), channel_id=1, source_target_pairs={{0,1},{1,0},{2,3},{3,2},{4,5},{5,4},{6,7},{7,6},{8,9},{9,8},{10,11... | collective-permute-start | bytes 7688 | tf_op jit(solution)/shard_map/ppermute | solution.py:406
  51.1 1.0 %collective-permute-done.9.refs_3_ = f32[1,640]{1,0:T(1,128)S(1)} collective-permute-done((f32[1,640]{1,0:T(1,128)S(1)}, f32[1,640]{1,0:T(1,128)S(1)}, u32[]{:S(2)}, u32[]{:S(2)}) %collective-permute-start.9) | collective-permute-done | bytes 2592 | tf_op jit(solution)/shard_map/ppermute | solution.py:406
  52.1 1.8 %collective-permute-done.8.refs_2_ = f32[1,640]{1,0:T(1,128)S(1)} collective-permute-done((f32[1,640]{1,0:T(1,128)S(1)}, f32[1,640]{1,0:T(1,128)S(1)}, u32[]{:S(2)}, u32[]{:S(2)}) %collective-permute-start.8) | collective-permute-done | bytes 2592 | tf_op jit(solution)/shard_map/ppermute | solution.py:406
  53.9 0.5 gather.1
  54.5 0.1 collective-permute-start.10
  54.5 1.4 %collective-permute-done.10.other_ref = f32[4,48,256]{2,1,0:T(8,128)S(1)} collective-permute-done((f32[4,48,256]{2,1,0:T(8,128)S(1)}, f32[4,48,256]{2,1,0:T(8,128)S(1)}, u32[]{:S(2)}, u32[]{:S(2)}) %collective-permute-start.10) | collective-permute-done | bytes 196640 | tf_op jit(solution)/shard_map/ppermute | solution.py:406
  56.0 2.5 %collective-permute-start.11 = (f32[48,256]{1,0:T(8,128)S(1)}, f32[48,256]{1,0:T(8,128)S(1)}, u32[]{:S(2)}, u32[]{:S(2)}) collective-permute-start(f32[48,256]{1,0:T(8,128)S(1)} %get-tuple-element.64), channel_id=1, source_target_pairs={{0,24},{4,28},{8,16},{12,20},{16,8},{20,12},{24,0},{28,4},{1,25},{... | collective-permute-start | bytes 147464 | tf_op jit(solution)/shard_map/ppermute | solution.py:406
  58.5 0.5 collective-permute-start.12
  59.0 0.5 collective-permute-start.13
  59.5 1.5 %collective-permute-done.11 = f32[48,256]{1,0:T(8,128)S(1)} collective-permute-done((f32[48,256]{1,0:T(8,128)S(1)}, f32[48,256]{1,0:T(8,128)S(1)}, u32[]{:S(2)}, u32[]{:S(2)}) %collective-permute-start.11) | collective-permute-done | bytes 49184 | tf_op jit(solution)/shard_map/ppermute | solution.py:406
  61.0 1.5 %collective-permute-done.12 = f32[48,256]{1,0:T(8,128)S(1)} collective-permute-done((f32[48,256]{1,0:T(8,128)S(1)}, f32[48,256]{1,0:T(8,128)S(1)}, u32[]{:S(2)}, u32[]{:S(2)}) %collective-permute-start.12) | collective-permute-done | bytes 49184 | tf_op jit(solution)/shard_map/ppermute | solution.py:406
  62.6 0.5 collective-permute-done.13
  63.1 1.5 %collective-permute-start.16 = (f32[48,256]{1,0:T(8,128)S(1)}, f32[48,256]{1,0:T(8,128)S(1)}, u32[]{:S(2)}, u32[]{:S(2)}) collective-permute-start(f32[48,256]{1,0:T(8,128)S(1)} %add_add_fusion.refs_0_), channel_id=1, source_target_pairs={{0,3},{1,2},{2,1},{3,0},{4,7},{5,6},{6,5},{7,4},{8,11},{9,10},{10,... | collective-permute-start | bytes 147464 | tf_op jit(solution)/shard_map/ppermute | solution.py:406
  64.6 0.9 %collective-permute-start.15 = (f32[48,256]{1,0:T(8,128)S(1)}, f32[48,256]{1,0:T(8,128)S(1)}, u32[]{:S(2)}, u32[]{:S(2)}) collective-permute-start(f32[48,256]{1,0:T(8,128)S(1)} %add_add_fusion.refs_0_), channel_id=1, source_target_pairs={{0,2},{1,3},{2,0},{3,1},{4,6},{5,7},{6,4},{7,5},{8,10},{9,11},{10,... | collective-permute-start | bytes 147464 | tf_op jit(solution)/shard_map/ppermute | solution.py:406
  65.5 2.0 %collective-permute-start.14 = (f32[48,256]{1,0:T(8,128)S(1)}, f32[48,256]{1,0:T(8,128)S(1)}, u32[]{:S(2)}, u32[]{:S(2)}) collective-permute-start(f32[48,256]{1,0:T(8,128)S(1)} %add_add_fusion.refs_0_), channel_id=1, source_target_pairs={{0,1},{1,0},{2,3},{3,2},{4,5},{5,4},{6,7},{7,6},{8,9},{9,8},{10,11... | collective-permute-start | bytes 147464 | tf_op jit(solution)/shard_map/ppermute | solution.py:406
  67.6 1.5 %collective-permute-done.16.refs_3_ = f32[48,256]{1,0:T(8,128)S(1)} collective-permute-done((f32[48,256]{1,0:T(8,128)S(1)}, f32[48,256]{1,0:T(8,128)S(1)}, u32[]{:S(2)}, u32[]{:S(2)}) %collective-permute-start.16) | collective-permute-done | bytes 49184 | tf_op jit(solution)/shard_map/ppermute | solution.py:406
  69.1 0.6 collective-permute-done.15.refs_2_
  69.7 0.5 collective-permute-done.14.refs_1_
  70.2 0.9 %update.1 = (f32[3,48,300]{2,1,0:T(8,128)}, f32[1,48]{1,0:T(1,128)}) custom-call(f32[3,48,300]{2,1,0:T(8,128)S(1)} %bitcast.12, f32[48,256]{1,0:T(8,128)S(1)} %add_add_fusion.refs_0_, f32[48,256]{1,0:T(8,128)S(1)} %collective-permute-done.14.refs_1_, f32[48,256]{1,0:T(8,128)S(1)} %collective-permute-done.15.refs_2_, ...), custom_call_target="tpu_custom_call" | custom-call | tf_op jit(solution)/shard_map/update/pallas_call | solution.py:392
  (27 shorter events, 0.1 us)
Async XLA Ops:
  0.6 3.8 %copy-start = (f32[48,3,300]{2,0,1:T(8,128)S(1)}, f32[48,3,300]{2,0,1:T(8,128)}, u32[]{:S(2)}) copy-start(f32[48,3,300]{2,0,1:T(8,128)} %param.8) | copy-start | bytes 518404
  0.6 3.7 %collective-permute-start = (f32[3,48,300]{2,1,0:T(8,128)}, f32[3,48,300]{2,1,0:T(8,128)S(1)}, u32[]{:S(2)}, u32[]{:S(2)}) collective-permute-start(f32[3,48,300]{2,1,0:T(8,128)} %bitcast.10), channel_id=1, source_target_pairs={{0,4},{4,0},{8,12},{12,8},{16,20},{20,16},{24,28},{28,24},{1,5},{5... | collective-permute-start | bytes 518408 | tf_op jit(solution)/shard_map/ppermute | solution.py:406
  1.2 1.7 %copy-start.2 = (f32[640,3,300]{0,2,1:T(8,128)S(1)}, f32[640,3,300]{0,2,1:T(8,128)}, u32[]{:S(2)}) copy-start(f32[640,3,300]{0,2,1:T(8,128)} %param.7) | copy-start | bytes 6912004
  2.8 5.8 %copy-start.1 = (bf16[11264,100]{0,1:T(8,128)(2,1)S(1)}, bf16[11264,100]{0,1:T(8,128)(2,1)}, u32[]{:S(2)}) copy-start(bf16[11264,100]{0,1:T(8,128)(2,1)} %param.13) | copy-start | bytes 6758404
  2.8 5.8 %copy-start.4 = (s32[2,11264]{1,0:T(2,128)S(1)}, s32[2,11264]{1,0:T(2,128)}, u32[]{:S(2)}) copy-start(s32[2,11264]{1,0:T(2,128)} %index_ref.1) | copy-start | bytes 270340
  2.8 5.8 %copy-start.5 = (f32[11264]{0:T(1024)S(1)}, f32[11264]{0:T(1024)}, u32[]{:S(2)}) copy-start(f32[11264]{0:T(1024)} %param.12) | copy-start | bytes 135172
  4.4 32.1 %collective-permute-start.3 = (f32[2,3,48,300]{3,2,1,0:T(8,128)S(1)}, f32[2,3,48,300]{3,2,1,0:T(8,128)S(1)}, u32[]{:S(2)}, u32[]{:S(2)}) collective-permute-start(f32[2,3,48,300]{3,2,1,0:T(8,128)S(1)} %pad_maximum_fusion.refs_0_), channel_id=1, source_target_pairs={{0,24},{4,28},{8,16},{12,20},{16,8},{20,12},{24,0},{28,4},{1,25},{... | collective-permute-start | bytes 1036808 | tf_op jit(solution)/shard_map/ppermute | solution.py:406
  8.0 28.6 %collective-permute-start.2 = (f32[2,3,48,300]{3,2,1,0:T(8,128)S(1)}, f32[2,3,48,300]{3,2,1,0:T(8,128)S(1)}, u32[]{:S(2)}, u32[]{:S(2)}) collective-permute-start(f32[2,3,48,300]{3,2,1,0:T(8,128)S(1)} %pad_maximum_fusion.refs_0_), channel_id=1, source_target_pairs={{0,16},{4,20},{8,24},{12,28},{16,0},{20,4},{24,8},{28,12},{1,17},{... | collective-permute-start | bytes 1036808 | tf_op jit(solution)/shard_map/ppermute | solution.py:406
  8.5 28.1 %collective-permute-start.1 = (f32[2,3,48,300]{3,2,1,0:T(8,128)S(1)}, f32[2,3,48,300]{3,2,1,0:T(8,128)S(1)}, u32[]{:S(2)}, u32[]{:S(2)}) collective-permute-start(f32[2,3,48,300]{3,2,1,0:T(8,128)S(1)} %pad_maximum_fusion.refs_0_), channel_id=1, source_target_pairs={{0,8},{4,12},{8,0},{12,4},{16,24},{20,28},{24,16},{28,20},{1,9},{5... | collective-permute-start | bytes 1036808 | tf_op jit(solution)/shard_map/ppermute | solution.py:406
  8.6 32.6 %copy-start.3 = (f32[640,3,300]{0,2,1:T(8,128)S(1)}, f32[640,3,300]{0,2,1:T(8,128)}, u32[]{:S(2)}) copy-start(f32[640,3,300]{0,2,1:T(8,128)} %param.7) | copy-start | bytes 6912004
  8.7 32.6 %copy-start.6 = (s32[640]{0:T(1024)S(1)}, s32[640]{0:T(1024)}, u32[]{:S(2)}) copy-start(s32[640]{0:T(1024)} %assigned_ref.1) | copy-start | bytes 7684
  8.7 32.6 %copy-start.7 = (s32[384]{0:T(512)S(1)}, s32[384]{0:T(512)}, u32[]{:S(2)}) copy-start(s32[384]{0:T(512)} %home_ref.1) | copy-start | bytes 4612
  36.6 7.8 %collective-permute-start.4 = (f32[128,128]{1,0:T(8,128)S(1)}, f32[128,128]{1,0:T(8,128)S(1)}, u32[]{:S(2)}, u32[]{:S(2)}) collective-permute-start(f32[128,128]{1,0:T(8,128)S(1)} %get-tuple-element.51), channel_id=1, source_target_pairs={{0,3},{1,2},{2,1},{3,0},{4,7},{5,6},{6,5},{7,4},{8,11},{9,10},{10,... | collective-permute-start | bytes 196616 | tf_op jit(solution)/shard_map/ppermute | solution.py:406
  40.6 5.4 %collective-permute-start.5 = (f32[128,128]{1,0:T(8,128)S(1)}, f32[128,128]{1,0:T(8,128)S(1)}, u32[]{:S(2)}, u32[]{:S(2)}) collective-permute-start(f32[128,128]{1,0:T(8,128)S(1)} %get-tuple-element.52), channel_id=1, source_target_pairs={{0,2},{1,3},{2,0},{3,1},{4,6},{5,7},{6,4},{7,5},{8,10},{9,11},{10,... | collective-permute-start | bytes 196616 | tf_op jit(solution)/shard_map/ppermute | solution.py:406
  40.6 5.4 %collective-permute-start.6 = (f32[128,128]{1,0:T(8,128)S(1)}, f32[128,128]{1,0:T(8,128)S(1)}, u32[]{:S(2)}, u32[]{:S(2)}) collective-permute-start(f32[128,128]{1,0:T(8,128)S(1)} %get-tuple-element.53), channel_id=1, source_target_pairs={{0,1},{1,0},{2,3},{3,2},{4,5},{5,4},{6,7},{7,6},{8,9},{9,8},{10,11... | collective-permute-start | bytes 196616 | tf_op jit(solution)/shard_map/ppermute | solution.py:406
  46.7 5.4 %collective-permute-start.9 = (f32[1,640]{1,0:T(1,128)S(1)}, f32[1,640]{1,0:T(1,128)S(1)}, u32[]{:S(2)}, u32[]{:S(2)}) collective-permute-start(f32[1,640]{1,0:T(1,128)S(1)} %get-tuple-element.60.refs_0_), channel_id=1, source_target_pairs={{0,3},{1,2},{2,1},{3,0},{4,7},{5,6},{6,5},{7,4},{8,11},{9,10},{10,... | collective-permute-start | bytes 7688 | tf_op jit(solution)/shard_map/ppermute | solution.py:406
  49.4 4.5 %collective-permute-start.8 = (f32[1,640]{1,0:T(1,128)S(1)}, f32[1,640]{1,0:T(1,128)S(1)}, u32[]{:S(2)}, u32[]{:S(2)}) collective-permute-start(f32[1,640]{1,0:T(1,128)S(1)} %get-tuple-element.60.refs_0_), channel_id=1, source_target_pairs={{0,2},{1,3},{2,0},{3,1},{4,6},{5,7},{6,4},{7,5},{8,10},{9,11},{10,... | collective-permute-start | bytes 7688 | tf_op jit(solution)/shard_map/ppermute | solution.py:406
  49.4 4.5 %collective-permute-start.7 = (f32[1,640]{1,0:T(1,128)S(1)}, f32[1,640]{1,0:T(1,128)S(1)}, u32[]{:S(2)}, u32[]{:S(2)}) collective-permute-start(f32[1,640]{1,0:T(1,128)S(1)} %get-tuple-element.60.refs_0_), channel_id=1, source_target_pairs={{0,1},{1,0},{2,3},{3,2},{4,5},{5,4},{6,7},{7,6},{8,9},{9,8},{10,11... | collective-permute-start | bytes 7688 | tf_op jit(solution)/shard_map/ppermute | solution.py:406
  54.5 1.5 %collective-permute-start.10 = (f32[4,48,256]{2,1,0:T(8,128)S(1)}, f32[4,48,256]{2,1,0:T(8,128)S(1)}, u32[]{:S(2)}, u32[]{:S(2)}) collective-permute-start(f32[4,48,256]{2,1,0:T(8,128)S(1)} %get-tuple-element.62), channel_id=1, source_target_pairs={{0,4},{4,0},{8,12},{12,8},{16,20},{20,16},{24,28},{28,24},{1,5},{5... | collective-permute-start | bytes 589832 | tf_op jit(solution)/shard_map/ppermute | solution.py:406
  56.0 5.1 %collective-permute-start.11 = (f32[48,256]{1,0:T(8,128)S(1)}, f32[48,256]{1,0:T(8,128)S(1)}, u32[]{:S(2)}, u32[]{:S(2)}) collective-permute-start(f32[48,256]{1,0:T(8,128)S(1)} %get-tuple-element.64), channel_id=1, source_target_pairs={{0,24},{4,28},{8,16},{12,20},{16,8},{20,12},{24,0},{28,4},{1,25},{... | collective-permute-start | bytes 147464 | tf_op jit(solution)/shard_map/ppermute | solution.py:406
  58.5 4.1 %collective-permute-start.12 = (f32[48,256]{1,0:T(8,128)S(1)}, f32[48,256]{1,0:T(8,128)S(1)}, u32[]{:S(2)}, u32[]{:S(2)}) collective-permute-start(f32[48,256]{1,0:T(8,128)S(1)} %get-tuple-element.65), channel_id=1, source_target_pairs={{0,16},{4,20},{8,24},{12,28},{16,0},{20,4},{24,8},{28,12},{1,17},{... | collective-permute-start | bytes 147464 | tf_op jit(solution)/shard_map/ppermute | solution.py:406
  59.0 4.1 %collective-permute-start.13 = (f32[48,256]{1,0:T(8,128)S(1)}, f32[48,256]{1,0:T(8,128)S(1)}, u32[]{:S(2)}, u32[]{:S(2)}) collective-permute-start(f32[48,256]{1,0:T(8,128)S(1)} %get-tuple-element.66), channel_id=1, source_target_pairs={{0,8},{4,12},{8,0},{12,4},{16,24},{20,28},{24,16},{28,20},{1,9},{5... | collective-permute-start | bytes 147464 | tf_op jit(solution)/shard_map/ppermute | solution.py:406
  63.1 6.0 %collective-permute-start.16 = (f32[48,256]{1,0:T(8,128)S(1)}, f32[48,256]{1,0:T(8,128)S(1)}, u32[]{:S(2)}, u32[]{:S(2)}) collective-permute-start(f32[48,256]{1,0:T(8,128)S(1)} %add_add_fusion.refs_0_), channel_id=1, source_target_pairs={{0,3},{1,2},{2,1},{3,0},{4,7},{5,6},{6,5},{7,4},{8,11},{9,10},{10,... | collective-permute-start | bytes 147464 | tf_op jit(solution)/shard_map/ppermute | solution.py:406
  64.6 5.0 %collective-permute-start.15 = (f32[48,256]{1,0:T(8,128)S(1)}, f32[48,256]{1,0:T(8,128)S(1)}, u32[]{:S(2)}, u32[]{:S(2)}) collective-permute-start(f32[48,256]{1,0:T(8,128)S(1)} %add_add_fusion.refs_0_), channel_id=1, source_target_pairs={{0,2},{1,3},{2,0},{3,1},{4,6},{5,7},{6,4},{7,5},{8,10},{9,11},{10,... | collective-permute-start | bytes 147464 | tf_op jit(solution)/shard_map/ppermute | solution.py:406
  65.5 4.6 %collective-permute-start.14 = (f32[48,256]{1,0:T(8,128)S(1)}, f32[48,256]{1,0:T(8,128)S(1)}, u32[]{:S(2)}, u32[]{:S(2)}) collective-permute-start(f32[48,256]{1,0:T(8,128)S(1)} %add_add_fusion.refs_0_), channel_id=1, source_target_pairs={{0,1},{1,0},{2,3},{3,2},{4,5},{5,4},{6,7},{7,6},{8,9},{9,8},{10,11... | collective-permute-start | bytes 147464 | tf_op jit(solution)/shard_map/ppermute | solution.py:406
